TPU v7x, 32 devices: a whole 2x2x4 slice. The times are simulated.
32 devices in a mesh: tile: 8 (over y, x, core), kern: 4 (over z).
Axes of the slice: x: 2, y: 2, z: 4, core: 2. Of those that a mesh axis runs over, the one named last changes fastest.
Arguments:
- mask_field: bfloat16 [512, 2048], P('tile'), may hold values from 0 to 1
- target_map: int32 [512, 2048], P('tile'), may hold values 0 or 1
- kernel_real: bfloat16 [4, 65, 65], P('kern'), may hold values from -0.09375 to 0.09375
- kernel_imag: bfloat16 [4, 65, 65], P('kern'), may hold values from -0.09375 to 0.09375
- socs_weight: float32 [4], replicated, may hold values from 0.05 to 1
- edge_pixel: int32 [32768], P(('tile', 'kern')), may hold values from 0 to 32767
- edge_owner: int32 [32768, 1], P(('tile', 'kern')), may hold values from 0 to 7; in each aligned block of 1024 rows (0 to 1023, 1024 to 2047, ...) at most 256 rows name the same one
- edge_slot: int32 [32768], P(('tile', 'kern')), may hold values from 0 to 255
- edge_weight: float32 [32768], P(('tile', 'kern')), may hold values from -1 to 1
Outputs:
- mask_grad: float32 [512, 2048], P('tile', 'kern')
- polygon_grad: float32 [2048], P('tile')
Inputs may be any that keep to these rules, and one draw needn't show every extreme that they name: `edge_owner`: at most 256 edge pixels of one device name the same owner band. `edge_pixel`: Row-major index within the device's own block of mask_grad.
All inputs are finite; a program needn't handle non-finite values. No bound on the sum of `target_map` on one device may be relied on, other than what follows from the above.
Results may differ from a plain program's by a relative error of at most 0.0028.
Values may be sent and summed in bfloat16 or wider, within the bound.
No kernel may reach another device: no remote copies, remote signals or barrier semaphores. Data moves between devices by JAX's collectives and lax.ppermute only.
A program may use at most 64 MiB of HBM per device.

v0:
```python
import jax
import jax.numpy as jnp
from jax import lax
from jax.sharding import PartitionSpec as P

POLY_DEV = 256


steepness = 8.0
threshold = 0.67


def extended(array, sides, width):
    for axis, dim in sides:
        size, length = (lax.axis_size(axis), array.shape[dim])
        up = [(i, (i + 1) % size) for i in range(size - 1)]
        down = [(j, i) for i, j in up]
        last = lax.slice_in_dim(array, length - width, length, axis=dim)
        first = lax.slice_in_dim(array, 0, width, axis=dim)
        before = lax.ppermute(last, axis, up)
        after = lax.ppermute(first, axis, down)
        array = jnp.concatenate([before, array, after], axis=dim)
    return array


def correlate(source, taps, out_rows):
    channels, in_rows, width = source.shape
    outputs = taps.shape[0]
    ksize = taps.shape[2]
    radius = (ksize - 1) // 2
    span = max(8, radius // 2)
    blocks = -(-out_rows // span)
    reach = span + 2 * radius
    extra = blocks * span + 2 * radius - in_rows
    padded = jnp.pad(source, ((0, 0), (0, extra), (0, 0)))
    row_index = (
        jnp.arange(blocks, dtype=jnp.int32)[:, None] * span
        + jnp.arange(reach, dtype=jnp.int32)[None]
    )
    windows = jnp.take(padded, row_index, axis=1)
    windows = windows.transpose(1, 0, 2, 3).reshape(blocks, channels * reach, width)
    offsets = (
        jnp.arange(reach, dtype=jnp.int32)[None, :, None]
        - jnp.arange(span, dtype=jnp.int32)[:, None, None]
    )
    onehot = (offsets == jnp.arange(ksize, dtype=jnp.int32)[None, None, :]).astype(jnp.bfloat16)
    band = jnp.einsum("yia,ocab->oycib", onehot, taps, preferred_element_type=jnp.float32).astype(
        jnp.bfloat16
    )
    band = band.reshape(outputs * span, channels * reach, ksize)
    result = lax.conv_general_dilated(
        windows,
        band,
        (1,),
        ((radius, radius),),
        dimension_numbers=("NCH", "OIH", "NCH"),
        preferred_element_type=jnp.float32,
    )
    result = (
        result.reshape(blocks, outputs, span, width)
        .transpose(1, 0, 2, 3)
        .reshape(outputs, blocks * span, width)
    )
    return result[:, :out_rows]


def resist_slope(intensity, target_piece, total_weight):
    resist = jax.nn.sigmoid(steepness * (intensity / total_weight - threshold))
    return (
        2.0
        * (resist - target_piece.astype(jnp.float32))
        * steepness
        * resist
        * (1.0 - resist)
        / total_weight
    )


def on_device(
    mask_field,
    target_map,
    kernel_real,
    kernel_imag,
    socs_weight,
    edge_pixel,
    edge_owner,
    edge_slot,
    edge_weight,
):
    row_count, tile_width = mask_field.shape
    kernel_count = kernel_real.shape[0]
    radius = (kernel_real.shape[1] - 1) // 2
    weights = lax.dynamic_slice_in_dim(
        socs_weight, lax.axis_index("kern") * kernel_count, kernel_count, 0
    )
    total_weight = jnp.sum(socs_weight)
    pair_weight = jnp.concatenate([weights, weights])
    stacked_taps = jnp.concatenate([kernel_real, kernel_imag], 0)
    forward_taps = stacked_taps[:, None]
    flipped = stacked_taps[None, :, ::-1, ::-1]
    padded = extended(mask_field, (("tile", 0),), radius)
    fields = correlate(padded[None], forward_taps, row_count)
    partial_value = jnp.sum(pair_weight[:, None, None] * fields * fields, 0)
    intensity = lax.psum(partial_value, "kern")
    slope = resist_slope(intensity, target_map, total_weight)
    product_scale = (2.0 * pair_weight)[:, None, None]
    products = (product_scale * slope[None] * fields).astype(jnp.bfloat16)
    beside_all = extended(products, (("tile", 1),), radius)
    grad_part = correlate(beside_all, flipped, row_count)[0]
    mask_grad = lax.psum_scatter(grad_part, "kern", scatter_dimension=1, tiled=True)
    local_grad = mask_grad.reshape(-1)
    edge_values = edge_weight * jnp.take(local_grad, edge_pixel)
    owner_tile = edge_owner[:, 0]
    tile_count = lax.axis_size("tile")
    edge_total = edge_pixel.shape[0]
    capacity = 2 * edge_total // tile_count
    owner_hit = (owner_tile[:, None] == jnp.arange(tile_count, dtype=jnp.int32)[None]).astype(
        jnp.int32
    )
    edge_rank = jnp.sum((jnp.cumsum(owner_hit, 0) - owner_hit) * owner_hit, 1)
    slot_place = owner_tile * capacity + edge_rank
    send_values = (
        jnp.zeros((tile_count * capacity,), jnp.float32)
        .at[slot_place]
        .set(edge_values)
        .reshape(tile_count, capacity)
    )
    send_slots = (
        jnp.zeros((tile_count * capacity,), jnp.float32)
        .at[slot_place]
        .set(edge_slot.astype(jnp.float32))
        .reshape(tile_count, capacity)
    )
    got_values, got_slots = (
        lax.all_to_all(send_values, "tile", split_axis=0, concat_axis=0, tiled=True),
        lax.all_to_all(send_slots, "tile", split_axis=0, concat_axis=0, tiled=True),
    )
    polygon_sums = jax.ops.segment_sum(
        got_values.reshape(-1), got_slots.reshape(-1).astype(jnp.int32), num_segments=POLY_DEV
    )
    polygon_grad = lax.psum(polygon_sums, "kern")
    return (mask_grad, polygon_grad)


def solution(mesh):
    placed = (
        P("tile", None),
        P("tile", None),
        P("kern", None, None),
        P("kern", None, None),
        P(),
        P(("tile", "kern")),
        P(("tile", "kern"), None),
        P(("tile", "kern")),
        P(("tile", "kern")),
    )
    return jax.shard_map(
        on_device,
        mesh=mesh,
        in_specs=placed,
        out_specs=(P("tile", "kern"), P("tile")),
        check_vma=False,
    )
```

profile of v0, /device:TPU:0, one launch (start us, length us, event | category | flops | bytes accessed | tf_op | source)
XLA Modules:
  0.0 578.8 jit_solution(17488771704943256851)
XLA Ops:
  8.2 2.4 collective-permute-start
  17.9 2.4 gather_fusion
  21.1 2.3 reshape.185
  25.4 4.2 copy.25
  29.6 173.2 %broadcast_select_fusion = f32[32,264,32]{2,0,1:T(8,128)} fusion(pred[32,264]{0,1:T(8,128)(4,1)S(1)} %copy-done.7, bf16[80,4,8,328]{0,2,1,3:T(8,128)(2,1)S(1)} %copy.25, bf16[32,80,65]{1,2,0:T(8,128)(2,1)S(1)} %bitcast.105), kind=kOutput, calls=%fused_computation.16 | convolution fusion | flops 2811764736 | bytes 3101952 | tf_op jit(solution)/shard_map/conv_general_dilated | solution.py:51
  202.8 4.0 copy.29
  211.7 40.8 %all-reduce.2.cloned.1.call-done = f32[64,2048]{1,0:T(8,128)} async-done(((f32[64,2048]{1,0:T(8,128)}), f32[64,2048]{1,0:T(8,128)}) %all-reduce.2.cloned.1.call-update) | async-done | bytes 524304 | tf_op jit(solution)/shard_map/psum | solution.py:104
  260.0 2.0 collective-permute-done.3
  263.5 14.4 %gather_fusion.1 = bf16[320,2,2048]{2,1,0:T(2,128)(2,1)} fusion(bf16[2,128,2048]{2,0,1:T(2,128)(2,1)S(1)} %pad_maximum_fusion, s32[1024]{0:T(1024)S(1)} %pad_clamp_fusion), kind=kCustom, calls=%fused_computation.1 | custom fusion | bytes 5244160 | tf_op jit(solution)/shard_map/jit(_take)/gather | solution.py:40
  277.8 3.4 copy_select_fusion
  283.1 5.5 reshape.192
  290.2 4.0 fusion.3
  294.2 9.3 %copy.33 = bf16[160,4,8,328]{0,2,1,3:T(8,128)(2,1)} copy(bf16[160,4,8,328]{3,2,0,1:T(8,128)(2,1)} %fusion.3) | data formatting | bytes 6717440 | tf_op jit(solution)/shard_map/conv_general_dilated | solution.py:51
  303.5 195.0 %fusion.10 = f32[32,264,16]{0,2,1:T(8,128)S(1)} fusion(bf16[16,160,65]{1,0,2:T(8,128)(2,1)S(1)} %reshape.179, bf16[160,4,8,328]{0,2,1,3:T(8,128)(2,1)} %copy.33, pred[32,264]{0,1:T(8,128)(4,1)S(1)} %copy-done.7), kind=kOutput, calls=%fused_computation.19 | convolution fusion | flops 2811629568 | bytes 4240640 | tf_op jit(solution)/shard_map/conv_general_dilated | solution.py:51
  501.2 2.3 reduce-window.6
  504.1 4.9 scatter_custom_fusion
  509.0 8.0 %all-to-all-start = ((f32[8,1,256]{2,1,0:T(1,128)}), f32[8,1,256]{2,1,0:T(1,128)S(1)}, u32[]{:S(2)}, u32[]{:S(2)}) async-start(f32[8,1,256]{2,1,0:T(1,128)} %bitcast.31), calls=%async_computation.1 | async-start | bytes 16384 | tf_op jit(solution)/shard_map/all_to_all | solution.py:136
  517.0 10.4 %reduce-scatter.2.cloned.1.call-done = f32[64,512]{1,0:T(8,128)} async-done(((f32[64,2048]{1,0:T(8,128)}), f32[64,512]{1,0:T(8,128)}) %reduce-scatter.2.cloned.1.call-update) | async-done | bytes 131088 | tf_op jit(solution)/shard_map/reduce_scatter | solution.py:110
  528.3 6.2 %gather_fusion.2 = f32[1024]{0:T(1024)S(1)} fusion(f32[32768]{0:T(1024)S(1)} %bitcast.97, s32[1024]{0:T(1024)S(1)} %fusion.32), kind=kCustom, calls=%fused_computation.2 | custom fusion | bytes 12288 | tf_op jit(solution)/shard_map/jit(_take)/gather | solution.py:112
  534.5 4.9 scatter_custom_fusion.1
  539.4 3.7 all-to-all-start.1
  543.1 4.7 all-to-all-done.1
  547.8 14.7 %scatter_custom_fusion.2 = f32[256]{0:T(256)S(1)} fusion(s32[2048]{0:T(1024)S(1)} %bitcast.112, f32[2048]{0:T(1024)S(1)} %bitcast.111, f32[]{:T(128)} %constant.45.clone.1), kind=kCustom, calls=%fused_computation.65 | custom fusion | flops 2048 | bytes 1028 | tf_op jit(solution)/shard_map/scatter-add | solution.py:138
  562.5 9.3 %psum.15 = f32[256]{0:T(256)} all-reduce(f32[256]{0:T(256)S(1)} %scatter_custom_fusion.2), channel_id=1, replica_groups=mesh['tile'=8,'kern'=4] {'kern'}, use_global_device_ids=true, to_apply=%region_10.11 | all-reduce | flops 256 | bytes 2048 | tf_op jit(solution)/shard_map/psum | solution.py:141
  (77 shorter events, 32.4 us)
Async XLA Ops:
  7.2 245.3 %all-reduce.2.cloned.1.call-start = ((), (), s32[]{:S(2)}) async-start(), calls=%async_computation.3 | async-start | bytes 1048576 | tf_op jit(solution)/shard_map/psum | solution.py:104
  8.2 8.7 %collective-permute-start = (bf16[32,2048]{1,0:T(8,128)(2,1)S(1)}, bf16[32,2048]{1,0:T(8,128)(2,1)S(1)}, u32[]{:S(2)}, u32[]{:S(2)}) collective-permute-start(bf16[32,2048]{1,0:T(8,128)(2,1)S(1)} %get-tuple-element.4), channel_id=1, source_target_pairs={{0,4},{4,8},{8,12},{12,16},{16,20},{20,24},{24,28},{1,5},{5,9},{9,... | collective-permute-start | bytes 393224 | tf_op jit(solution)/shard_map/ppermute | solution.py:20
  10.6 6.3 %collective-permute-start.1 = (bf16[32,2048]{1,0:T(8,128)(2,1)S(1)}, bf16[32,2048]{1,0:T(8,128)(2,1)S(1)}, u32[]{:S(2)}, u32[]{:S(2)}) collective-permute-start(bf16[32,2048]{1,0:T(8,128)(2,1)S(1)} %get-tuple-element.5), channel_id=1, source_target_pairs={{4,0},{8,4},{12,8},{16,12},{20,16},{24,20},{28,24},{5,1},{9,5},{13... | collective-permute-start | bytes 393224 | tf_op jit(solution)/shard_map/ppermute | solution.py:21
  25.4 4.2 copy-start
  25.4 4.2 copy-start.7
  207.8 1.7 copy-start.6
  208.4 44.1 %copy-start.1 = (s32[64,2048]{1,0:T(8,128)S(1)}, s32[64,2048]{1,0:T(8,128)}, u32[]{:S(2)}) copy-start(s32[64,2048]{1,0:T(8,128)} %param.10) | copy-start | bytes 1572868
  209.5 317.9 %reduce-scatter.2.cloned.1.call-start = ((), (), s32[]{:S(2)}) async-start(), calls=%async_computation.4 | async-start | bytes 655360 | tf_op jit(solution)/shard_map/reduce_scatter | solution.py:110
  255.5 4.4 collective-permute-start.2
  256.8 5.1 collective-permute-start.3
  499.6 1.7 copy-start.2
  499.6 4.4 copy-start.4
  499.6 17.4 %copy-start.3 = (s32[1024]{0:T(1024)S(1)}, s32[1024]{0:T(1024)}, u32[]{:S(2)}) copy-start(s32[1024]{0:T(1024)} %param.14) | copy-start | bytes 12292
  501.2 33.3 %copy-start.5 = (f32[1024]{0:T(1024)S(1)}, f32[1024]{0:T(1024)}, u32[]{:S(2)}) copy-start(f32[1024]{0:T(1024)} %param.17) | copy-start | bytes 12292
  509.0 30.4 %all-to-all-start = ((f32[8,1,256]{2,1,0:T(1,128)}), f32[8,1,256]{2,1,0:T(1,128)S(1)}, u32[]{:S(2)}, u32[]{:S(2)}) async-start(f32[8,1,256]{2,1,0:T(1,128)} %bitcast.31), calls=%async_computation.1 | async-start | bytes 16384 | tf_op jit(solution)/shard_map/all_to_all | solution.py:136
  539.4 8.4 %all-to-all-start.1 = ((f32[8,1,256]{2,1,0:T(1,128)}), f32[8,1,256]{2,1,0:T(1,128)S(1)}, u32[]{:S(2)}, u32[]{:S(2)}) async-start(f32[8,1,256]{2,1,0:T(1,128)} %bitcast.33), calls=%async_computation.2 | async-start | bytes 16384 | tf_op jit(solution)/shard_map/all_to_all | solution.py:135
Sparse Core Ops, SparseCore 0:
  209.6 42.8 all-reduce.1
  501.3 26.0 reduce-scatter.1
where the time goes:
time: 581 us; the launch traced here: 579 us
  matrix products  370 us (64%)
  local copies, waits for them, and re-layouts  74.4 us (13%)
  waiting for transfers between devices  58 us (10%)
  other arithmetic  34.9 us (6%)
  starting transfers between devices  18 us (3%)
  between operations  14.7 us (3%)
  blocking collectives  9.28 us (2%)
    conv_general_dilated x2, matrix products, correlate(): lax.conv_general_dilated(windows, band, (1,), ((radius, radius),), dimens...  368 us
    psum x1, waiting for transfers between devices, on_device(): intensity = lax.psum(partial_value, 'kern')  40.8 us
    conv_general_dilated x14, local copies, waits for them, and re-layouts, correlate(): lax.conv_general_dilated(windows, band, (1,), ((radius, radius),), dimens...  31.4 us
    gather x2, local copies, waits for them, and re-layouts, correlate(): windows = jnp.take(padded, row_index, axis=1)  16.8 us
    scatter-add x1, other arithmetic, on_device(): jax.ops.segment_sum(got_values.reshape(-1), got_slots.reshape(-1).astype(...  14.7 us
  transfers between devices with their start and end apart: 8, of which 4 were waited for; matrix products, arithmetic and copies ran while one was open for 5% of the time, Pallas kernels for 0%

commit v1 on v0

v1 whole, which is shorter than its diff:
```python
import functools

import jax
import jax.numpy as jnp
from jax import lax
from jax.experimental import pallas as pl
from jax.experimental.pallas import tpu as pltpu
from jax.sharding import PartitionSpec as P

POLY_DEV = 256

steepness = 8.0
threshold = 0.67

F32 = jnp.float32
BF16 = jnp.bfloat16
LANES = 128
SIDE = 128
VMEM = pl.BlockSpec(memory_space=pltpu.VMEM)
SMEM = pl.BlockSpec(memory_space=pltpu.SMEM)


def pack_kernel(block, pos_ref, mask_ref, target_ref, real_ref, imag_ref, out_ref, rest_ref, taps_ref, square):
    rows, width = mask_ref.shape
    half = rows // 2
    first = pos_ref[0] * block
    left = jnp.maximum(first - SIDE, 0)
    right = jnp.minimum(first + block, width - SIDE)
    has_left = first > 0
    has_right = first + block < width
    pieces = (
        (pl.ds(pl.multiple_of(left, LANES), SIDE), slice(0, SIDE), has_left),
        (pl.ds(pl.multiple_of(first, LANES), block), slice(SIDE, SIDE + block), None),
        (pl.ds(pl.multiple_of(right, LANES), SIDE), slice(SIDE + block, 2 * SIDE + block), has_right),
    )
    for source, place, inside in pieces:
        mask = mask_ref[:, source]
        if inside is not None:
            mask = jnp.where(inside, mask.astype(F32), 0.0).astype(BF16)
        out_ref[0:rows, place] = mask
        target = target_ref[:, source].astype(F32).astype(BF16)
        out_ref[rows : rows + half, place] = target[:half]
        rest_ref[:, place] = target[half:]
    ksize = real_ref.shape[1]
    count = real_ref.shape[0]
    for kernel in range(count):
        for part, ref in enumerate((real_ref, imag_ref)):
            square[...] = jnp.zeros_like(square)
            square[0:ksize, 0:ksize] = ref[kernel].astype(F32)
            taps_ref[2 * kernel + part] = square[...].T[: taps_ref.shape[1]].astype(BF16)


def field_kernel(
    block, width, ksize, n_sets, pos_ref, weight_ref, own_ref, next_ref, rest_ref, *refs
):
    tap_refs = refs[:n_sets]
    here_ref, there_ref = refs[n_sets : n_sets + 2]
    taps32, mask_t, target_t, band, fields, products, total = refs[n_sets + 2 :]
    radius = (ksize - 1) // 2
    per_set = tap_refs[0].shape[0]
    pairs = n_sets * per_set // 2
    rows = here_ref.shape[0]
    half = rows // 2
    window = 2 * rows
    span = block + 2 * radius
    chunks = (ksize - 1) // 8
    kern_at = pos_ref[0]
    last = pos_ref[1]

    for index, ref in enumerate(tap_refs):
        taps32[index * per_set : (index + 1) * per_set] = ref[...].astype(F32)
    for piece in range((block + 2 * SIDE) // LANES):
        lanes = slice(piece * LANES, (piece + 1) * LANES)
        both = jnp.concatenate([own_ref[0:rows, lanes], next_ref[0:rows, lanes]], 0)
        mask_t[lanes, :] = both.astype(F32).T
        one = jnp.concatenate([rest_ref[:, lanes], next_ref[rows : rows + half, lanes]], 0)
        target_t[lanes, :] = jnp.concatenate([one, one], 0).astype(F32).T

    out_row = lax.broadcasted_iota(jnp.int32, (rows, window), 0) < half
    in_row = lax.broadcasted_iota(jnp.int32, (rows, window), 1) < rows
    keep = jnp.logical_or(out_row == in_row, last == 0)
    keep = keep.astype(F32)

    def toeplitz(component, column_rows, j):
        row = jnp.broadcast_to(column_rows[j : j + 1], (rows, window))
        return (pltpu.roll(row, 0, 1, stride=1, stride_axis=0) * keep).astype(BF16)

    def build(chunk, carry):
        start = pl.multiple_of(chunk * 8, 8)
        for component in range(2 * pairs):
            column_rows = taps32[component, pl.ds(start, 8), :]
            for j in range(8):
                band[chunk, component * rows : (component + 1) * rows, j * window : (j + 1) * window] = (
                    toeplitz(component, column_rows, j)
                )
        return carry

    lax.fori_loop(0, chunks, build, 0)
    for component in range(2 * pairs):
        column_rows = taps32[component, chunks * 8 : chunks * 8 + 8, :]
        band[chunks, component * rows : (component + 1) * rows, 0:window] = toeplitz(component, column_rows, 0)

    nt = (((1,), (1,)), ((), ()))
    base = SIDE - 2 * radius
    tail = mask_t[base + chunks * 8 : base + chunks * 8 + span, :].astype(BF16)
    fields[...] = lax.dot_general(tail, band[chunks, :, 0:window], nt, preferred_element_type=F32)

    def forward(chunk, carry):
        start = pl.multiple_of(base + chunk * 8, 8)
        parts = [mask_t[pl.ds(start + j, span), :].astype(BF16) for j in range(8)]
        left = jnp.concatenate(parts, 1)
        fields[...] += lax.dot_general(left, band[chunk], nt, preferred_element_type=F32)
        return carry

    lax.fori_loop(0, chunks, forward, 0)

    weights = []
    for index in range(n_sets):
        source = lax.rem(kern_at - index + n_sets, n_sets)
        for kernel in range(per_set // 2):
            weights.append(weight_ref[source * (per_set // 2) + kernel])
    total_weight = weight_ref[0]
    for kernel in range(1, pairs):
        total_weight = total_weight + weight_ref[kernel]
    total_weight = jnp.full((1, window), total_weight, F32)
    intensity = jnp.zeros((span, window), F32)
    for kernel in range(pairs):
        field = fields[:, kernel * window : (kernel + 1) * window]
        intensity = intensity + weights[kernel] * field * field
    intensity = intensity + pltpu.roll(intensity, rows, 1)
    resist = jax.nn.sigmoid(steepness * (intensity / total_weight - threshold))
    target = target_t[SIDE - radius : SIDE - radius + span, :]
    slope = 2.0 * (resist - target) * steepness * resist * (1.0 - resist) / total_weight
    column = kern_at * block - radius + lax.broadcasted_iota(jnp.int32, (span, window), 0)
    slope = jnp.where(jnp.logical_and(column >= 0, column < width), slope, 0.0)
    for kernel in range(pairs):
        lanes = slice(kernel * window, (kernel + 1) * window)
        products[:, lanes] = ((2.0 * weights[kernel]) * slope * fields[:, lanes]).astype(BF16)

    total[...] = jnp.zeros_like(total)
    total[chunks * 8 : chunks * 8 + span, :] = jnp.dot(
        products[...], band[chunks, :, 0:window], preferred_element_type=F32
    )

    def adjoint(chunk, carry):
        start = pl.multiple_of(chunk * 8, 8)
        for j in range(0, 8, 2):
            two = jnp.dot(
                products[...], band[chunk, :, j * window : (j + 2) * window], preferred_element_type=F32
            )
            total[pl.ds(start + j, span), :] += two[:, :window]
            total[pl.ds(start + j + 1, span), :] += two[:, window:]
        return carry

    lax.fori_loop(0, chunks, adjoint, 0)
    for piece in range(block // LANES):
        lanes = slice(piece * LANES, (piece + 1) * LANES)
        turned = total[2 * radius + piece * LANES : 2 * radius + (piece + 1) * LANES, :].T
        here_ref[:, lanes] = turned[:rows]
        there_ref[:, lanes] = turned[rows:]


def split3(value):
    high = value.astype(BF16)
    rest = value - high.astype(F32)
    middle = rest.astype(BF16)
    low = (rest - middle.astype(F32)).astype(BF16)
    return high, middle, low


def edge_kernel(here_ref, came_ref, pixel_ref, owner_ref, slot_ref, weight_ref, grad_ref, sums_ref):
    rows, block = grad_ref.shape
    tiles, slots = sums_ref.shape
    grad = here_ref[...] + came_ref[...]
    grad_ref[...] = grad
    edges = pixel_ref.shape[1]
    pixel = pixel_ref[...]
    row = pixel // block
    col = pixel - row * block
    row_hit = (lax.broadcasted_iota(jnp.int32, (rows, edges), 0) == row).astype(F32).astype(BF16)
    col_hit = lax.broadcasted_iota(jnp.int32, (block, edges), 0) == col
    tn = (((0,), (0,)), ((), ()))
    picked = jnp.zeros((block, edges), F32)
    for part in split3(grad):
        picked = picked + lax.dot_general(part, row_hit, tn, preferred_element_type=F32)
    value = jnp.sum(jnp.where(col_hit, picked, 0.0), 0, keepdims=True) * weight_ref[...]
    owner_hit = lax.broadcasted_iota(jnp.int32, (tiles, edges), 0) == owner_ref[...]
    slot_hit = (lax.broadcasted_iota(jnp.int32, (slots, edges), 0) == slot_ref[...]).astype(F32).astype(BF16)
    nt = (((1,), (1,)), ((), ()))
    spread = jnp.where(owner_hit, value, 0.0)
    sums = jnp.zeros((tiles, slots), F32)
    for part in split3(spread):
        sums = sums + lax.dot_general(part, slot_hit, nt, preferred_element_type=F32)
    sums_ref[...] = sums


def on_device(
    mask_field,
    target_map,
    kernel_real,
    kernel_imag,
    socs_weight,
    edge_pixel,
    edge_owner,
    edge_slot,
    edge_weight,
):
    rows, width = mask_field.shape
    count, ksize = kernel_real.shape[:2]
    tiles, kerns = lax.axis_size("tile"), lax.axis_size("kern")
    block = width // kerns
    radius = (ksize - 1) // 2
    span = block + 2 * radius
    whole = block + 2 * SIDE
    kern_at = lax.axis_index("kern")
    tile_at = lax.axis_index("tile")
    place = jnp.stack([kern_at, (tile_at == tiles - 1).astype(jnp.int32)]).astype(jnp.int32)
    tap_rows = -(-ksize // 8) * 8
    own, rest, taps = pl.pallas_call(
        functools.partial(pack_kernel, block),
        out_shape=(
            jax.ShapeDtypeStruct((rows + rows // 2, whole), BF16),
            jax.ShapeDtypeStruct((rows // 2, whole), BF16),
            jax.ShapeDtypeStruct((2 * count, tap_rows, LANES), BF16),
        ),
        in_specs=[SMEM] + [VMEM] * 4,
        out_specs=(VMEM,) * 3,
        scratch_shapes=[pltpu.VMEM((LANES, LANES), F32)],
        name="pack",
    )(place, mask_field, target_map, kernel_real, kernel_imag)

    following = lax.ppermute(own, "tile", [(i, (i - 1) % tiles) for i in range(tiles)])
    tap_sets = [taps] + [
        lax.ppermute(taps, "kern", [(i, (i + step) % kerns) for i in range(kerns)])
        for step in range(1, kerns)
    ]
    components = 2 * count * kerns
    chunks = (ksize - 1) // 8
    band_bytes = (chunks + 1) * components * rows * 8 * LANES * 2
    here, there = pl.pallas_call(
        functools.partial(field_kernel, block, width, ksize, kerns),
        out_shape=(jax.ShapeDtypeStruct((rows, block), F32),) * 2,
        in_specs=[SMEM, SMEM] + [VMEM] * (3 + kerns),
        out_specs=(VMEM,) * 2,
        scratch_shapes=[
            pltpu.VMEM((components, tap_rows, LANES), F32),
            pltpu.VMEM((whole, LANES), F32),
            pltpu.VMEM((whole, LANES), F32),
            pltpu.VMEM((chunks + 1, components * rows, 8 * LANES), BF16),
            pltpu.VMEM((span, components * rows), F32),
            pltpu.VMEM((span, components * rows), BF16),
            pltpu.VMEM((span + 2 * radius, LANES), F32),
        ],
        compiler_params=pltpu.CompilerParams(vmem_limit_bytes=band_bytes + (20 << 20)),
        name="fields",
    )(place, socs_weight, own, following, rest, *tap_sets)
    came = lax.ppermute(there, "tile", [(i, (i + 1) % tiles) for i in range(tiles)])
    mask_grad, sums = pl.pallas_call(
        edge_kernel,
        out_shape=(
            jax.ShapeDtypeStruct((rows, block), F32),
            jax.ShapeDtypeStruct((tiles, POLY_DEV), F32),
        ),
        in_specs=[VMEM] * 6,
        out_specs=(VMEM,) * 2,
        name="edges",
    )(
        here,
        came,
        edge_pixel[None, :],
        edge_owner.reshape(1, -1),
        edge_slot[None, :],
        edge_weight[None, :],
    )
    spread = jnp.repeat(sums, kerns, axis=0)
    got = lax.all_to_all(spread, ("tile", "kern"), 0, 0, tiled=True)
    return (mask_grad, jnp.sum(got, 0))


def solution(mesh):
    placed = (
        P("tile", None),
        P("tile", None),
        P("kern", None, None),
        P("kern", None, None),
        P(),
        P(("tile", "kern")),
        P(("tile", "kern"), None),
        P(("tile", "kern")),
        P(("tile", "kern")),
    )
    return jax.shard_map(
        on_device,
        mesh=mesh,
        in_specs=placed,
        out_specs=(P("tile", "kern"), P("tile")),
        check_vma=False,
    )
```

time: 581 us -> 60.2 us (0.10)
  matrix products: 370 us -> 0 us
  local copies, waits for them, and re-layouts: 74.4 us -> 4.51 us
  waiting for transfers between devices: 58 us -> 10.2 us
  other arithmetic: 34.9 us -> 1.21 us
  Pallas kernels: 0 us -> 26.2 us
  between operations: 14.7 us -> 0.68 us
  starting transfers between devices: 18 us -> 7.95 us
    conv_general_dilated x2 -> x0, matrix products: 368 us -> none  [correlate(): lax.conv_general_dilated(windows, band, (1,), ((radius, radius),), dimens...]
    psum x1 -> x0, waiting for transfers between devices: 40.8 us -> none  [on_device(): intensity = lax.psum(partial_value, 'kern')]
    conv_general_dilated x14 -> x0, local copies, waits for them, and re-layouts: 31.4 us -> none  [correlate(): lax.conv_general_dilated(windows, band, (1,), ((radius, radius),), dimens...]
    pallas_call x0 -> x3, Pallas kernels: none -> 26.2 us  [the longest x1 20.8 us: on_device(): pl.pallas_call(functools.partial(field_kernel, block, width, ksize, kerns...]
    gather x3 -> x0, local copies, waits for them, and re-layouts: 23 us -> none  [the longest x2 16.8 us: correlate(): windows = jnp.take(padded, row_index, axis=1)]
    scatter-add x1 -> x0, other arithmetic: 14.7 us -> none  [on_device(): jax.ops.segment_sum(got_values.reshape(-1), got_slots.reshape(-1).astype(...]
    all_to_all x2 -> x0, starting transfers between devices: 11.7 us -> none  [the longest x1 8.01 us: on_device(): lax.all_to_all(send_slots, 'tile', split_axis=0, concat_axis=0, tiled=True)]
    reduce_scatter x1 -> x0, waiting for transfers between devices: 10.4 us -> none  [on_device(): lax.psum_scatter(grad_part, 'kern', scatter_dimension=1, tiled=True)]
  transfers between devices with their start and end apart: 8 -> 5, of which waited for: 4 -> 4; matrix products, arithmetic and copies ran while one was open for 5% -> 0% of each run, Pallas kernels for 0% -> 0%
where the time goes in v1:
time: 60.2 us; the launch traced here: 59.8 us
  Pallas kernels  26.2 us (44%)
  waiting for transfers between devices  10.2 us (17%)
  blocking collectives  8.99 us (15%)
  starting transfers between devices  7.95 us (13%)
  local copies, waits for them, and re-layouts  4.51 us (7%)
  other arithmetic  1.21 us (2%)
  between operations  0.68 us (1%)
    pallas_call x1, Pallas kernels, on_device(): pl.pallas_call(functools.partial(field_kernel, block, width, ksize, kerns...  20.8 us
    all_to_all x1, blocking collectives, on_device(): got = lax.all_to_all(spread, ('tile', 'kern'), 0, 0, tiled=True)  8.99 us
    ppermute x1, waiting for transfers between devices, on_device(): lax.ppermute(there, 'tile', [(i, (i + 1) % tiles) for i in range(tiles)])  5.29 us
    ppermute x3, waiting for transfers between devices, on_device(): lax.ppermute(taps, 'kern', [(i, (i + step) % kerns) for i in range(kerns)])  4.96 us
    ppermute x3, starting transfers between devices, on_device(): lax.ppermute(taps, 'kern', [(i, (i + step) % kerns) for i in range(kerns)])  4.62 us
    unnamed x14, local copies, waits for them, and re-layouts  3.77 us
    pallas_call x1, Pallas kernels, on_device(): pl.pallas_call(edge_kernel, out_shape=(jax.ShapeDtypeStruct((rows, block)...  3.63 us
    ppermute x1, starting transfers between devices, on_device(): lax.ppermute(own, 'tile', [(i, (i - 1) % tiles) for i in range(tiles)])  3.33 us
  transfers between devices with their start and end apart: 5, of which 4 were waited for; matrix products, arithmetic and copies ran while one was open for 0% of the time, Pallas kernels for 0%

profile of v1, /device:TPU:0, one launch (start us, length us, event | category | flops | bytes accessed | tf_op | source)
XLA Modules:
  0.0 59.8 jit_solution(3658022523384274338)
XLA Ops:
  0.6 0.6 pad_add_fusion.pos_ref
  1.2 1.8 %pack.1 = (bf16[96,768]{1,0:T(8,128)(2,1)}, bf16[32,768]{1,0:T(8,128)(2,1)}, bf16[2,72,128]{2,1,0:T(8,128)(2,1)}) custom-call(s32[2]{0:T(128)} %pad_add_fusion.pos_ref, bf16[64,2048]{1,0:T(8,128)(2,1)} %mask_ref.1, s32[64,2048]{1,0:T(8,128)} %target_ref.1, bf16[1,65,65]{2,1,0:T(8,128)(2,1)} %real_ref.1, bf16[1,65,65]{2,1,0:T(8,128)(2,1)} %imag_ref.1), custom_call_target="tpu_custom_call" | custom-call | tf_op jit(solution)/shard_map/pack/pallas_call | solution.py:219
  3.1 3.3 %collective-permute-start = (bf16[96,768]{1,0:T(8,128)(2,1)}, bf16[96,768]{1,0:T(8,128)(2,1)S(1)}, u32[]{:S(2)}, u32[]{:S(2)}) collective-permute-start(bf16[96,768]{1,0:T(8,128)(2,1)} %get-tuple-element.9.own_ref), channel_id=1, source_target_pairs={{0,28},{4,0},{8,4},{12,8},{16,12},{20,16},{24,20},{28,24},{1,29},{... | collective-permute-start | bytes 442376 | tf_op jit(solution)/shard_map/ppermute | solution.py:232
  6.4 3.6 %collective-permute-start.3 = (bf16[2,72,128]{2,1,0:T(8,128)(2,1)}, bf16[2,72,128]{2,1,0:T(8,128)(2,1)S(1)}, u32[]{:S(2)}, u32[]{:S(2)}) collective-permute-start(bf16[2,72,128]{2,1,0:T(8,128)(2,1)} %get-tuple-element.11.refs_0_), channel_id=1, source_target_pairs={{0,3},{1,0},{2,1},{3,2},{4,7},{5,4},{6,5},{7,6},{8,11},{9,8},{10,9... | collective-permute-start | bytes 110600 | tf_op jit(solution)/shard_map/ppermute | solution.py:234
  10.0 0.0 collective-permute-start.2
  10.0 1.0 %collective-permute-start.1 = (bf16[2,72,128]{2,1,0:T(8,128)(2,1)}, bf16[2,72,128]{2,1,0:T(8,128)(2,1)S(1)}, u32[]{:S(2)}, u32[]{:S(2)}) collective-permute-start(bf16[2,72,128]{2,1,0:T(8,128)(2,1)} %get-tuple-element.11.refs_0_), channel_id=1, source_target_pairs={{0,1},{1,2},{2,3},{3,0},{4,5},{5,6},{6,7},{7,4},{8,9},{9,10},{10,1... | collective-permute-start | bytes 110600 | tf_op jit(solution)/shard_map/ppermute | solution.py:234
  11.0 0.9 %collective-permute-done.3.refs_3_ = bf16[2,72,128]{2,1,0:T(8,128)(2,1)S(1)} collective-permute-done((bf16[2,72,128]{2,1,0:T(8,128)(2,1)}, bf16[2,72,128]{2,1,0:T(8,128)(2,1)S(1)}, u32[]{:S(2)}, u32[]{:S(2)}) %collective-permute-start.3) | collective-permute-done | bytes 36896 | tf_op jit(solution)/shard_map/ppermute | solution.py:234
  12.0 3.1 %collective-permute-done.2.refs_2_ = bf16[2,72,128]{2,1,0:T(8,128)(2,1)S(1)} collective-permute-done((bf16[2,72,128]{2,1,0:T(8,128)(2,1)}, bf16[2,72,128]{2,1,0:T(8,128)(2,1)S(1)}, u32[]{:S(2)}, u32[]{:S(2)}) %collective-permute-start.2) | collective-permute-done | bytes 36896 | tf_op jit(solution)/shard_map/ppermute | solution.py:234
  15.1 0.9 %collective-permute-done.1.refs_1_ = bf16[2,72,128]{2,1,0:T(8,128)(2,1)S(1)} collective-permute-done((bf16[2,72,128]{2,1,0:T(8,128)(2,1)}, bf16[2,72,128]{2,1,0:T(8,128)(2,1)S(1)}, u32[]{:S(2)}, u32[]{:S(2)}) %collective-permute-start.1) | collective-permute-done | bytes 36896 | tf_op jit(solution)/shard_map/ppermute | solution.py:234
  16.0 0.0 collective-permute-done.next_ref
  16.0 0.0 copy-done.4
  16.0 0.0 copy-done.5
  16.0 0.9 %copy-done = bf16[96,768]{1,0:T(8,128)(2,1)S(1)} copy-done((bf16[96,768]{1,0:T(8,128)(2,1)S(1)}, bf16[96,768]{1,0:T(8,128)(2,1)}, u32[]{:S(2)}) %copy-start) | copy-done | bytes 147480
  16.9 0.8 %copy-done.2 = bf16[32,768]{1,0:T(8,128)(2,1)S(1)} copy-done((bf16[32,768]{1,0:T(8,128)(2,1)S(1)}, bf16[32,768]{1,0:T(8,128)(2,1)}, u32[]{:S(2)}) %copy-start.2) | copy-done | bytes 49176
  17.7 0.8 %copy-done.3 = bf16[2,72,128]{2,1,0:T(8,128)(2,1)S(1)} copy-done((bf16[2,72,128]{2,1,0:T(8,128)(2,1)S(1)}, bf16[2,72,128]{2,1,0:T(8,128)(2,1)}, u32[]{:S(2)}) %copy-start.3) | copy-done | bytes 36888
  18.5 20.8 %fields.1 = (f32[64,512]{1,0:T(8,128)S(1)}, f32[64,512]{1,0:T(8,128)S(1)}) custom-call(s32[2]{0:T(128)S(1)} %copy-done.4, f32[4]{0:T(128)S(1)} %copy-done.5, bf16[96,768]{1,0:T(8,128)(2,1)S(1)} %copy-done, bf16[96,768]{1,0:T(8,128)(2,1)S(1)} %collective-permute-done.next_ref, bf16[32,768]{1,0:T(8,128)(2,1)S(1)} %copy-done.2, ...), custom_call_target="tpu_custom_call" | custom-call | tf_op jit(solution)/shard_map/fields/pallas_call | solution.py:240
  39.2 0.6 %copy-done.1 = f32[64,512]{1,0:T(8,128)} copy-done((f32[64,512]{1,0:T(8,128)}, f32[64,512]{1,0:T(8,128)S(1)}, u32[]{:S(2)}) %copy-start.1) | copy-done | bytes 131096
  39.9 0.0 collective-permute-start.4
  39.9 5.3 %collective-permute-done.4.came_ref = f32[64,512]{1,0:T(8,128)S(1)} collective-permute-done((f32[64,512]{1,0:T(8,128)S(1)}, f32[64,512]{1,0:T(8,128)S(1)}, u32[]{:S(2)}, u32[]{:S(2)}) %collective-permute-start.4) | collective-permute-done | bytes 131104 | tf_op jit(solution)/shard_map/ppermute | solution.py:257
  45.2 0.6 %copy-done.6 = f32[64,512]{1,0:T(8,128)} copy-done((f32[64,512]{1,0:T(8,128)}, f32[64,512]{1,0:T(8,128)S(1)}, u32[]{:S(2)}) %copy-start.6) | copy-done | bytes 131096
  45.8 3.6 %edges.1 = (f32[64,512]{1,0:T(8,128)}, f32[8,256]{1,0:T(8,128)}) custom-call(f32[64,512]{1,0:T(8,128)} %copy-done.1, f32[64,512]{1,0:T(8,128)} %copy-done.6, s32[1,1024]{1,0:T(1,128)} %bitcast.6, s32[1,1024]{1,0:T(1,128)} %bitcast.7, s32[1,1024]{1,0:T(1,128)} %bitcast.8, f32[1,1024]{1,0:T(1,128)} %bitcast.9), custom_call_target="tpu_custom_call" | custom-call | tf_op jit(solution)/shard_map/edges/pallas_call | solution.py:258
  49.5 0.7 %broadcast_in_dim.15 = f32[8,4,256]{2,1,0:T(4,128)S(1)} broadcast(f32[8,256]{1,0:T(8,128)} %get-tuple-element.15), dimensions={0,2} | broadcast | bytes 40960 | tf_op jit(solution)/shard_map/broadcast_in_dim | solution.py:275
  50.2 9.0 %all_to_all.9 = f32[32,1,256]{2,1,0:T(1,128)S(1)} all-to-all(f32[32,1,256]{2,1,0:T(1,128)S(1)} %all_to_all.6), channel_id=1, replica_groups=mesh['tile'=8,'kern'=4] {'tile','kern'}, dimensions={0} | all-to-all | bytes 65536 | tf_op jit(solution)/shard_map/all_to_all | solution.py:276
  59.2 0.6 %reduce_sum.9 = f32[256]{0:T(256)} reduce(f32[32,1,256]{2,1,0:T(1,128)S(1)} %all_to_all.9, f32[]{:T(128)} %constant.12.clone.1), dimensions={0,1}, to_apply=%region_0.0 | reduce | flops 7936 | bytes 33796 | tf_op jit(solution)/shard_map/reduce_sum | solution.py:277
  (8 shorter events, 0.1 us)
Async XLA Ops:
  3.1 12.9 %collective-permute-start = (bf16[96,768]{1,0:T(8,128)(2,1)}, bf16[96,768]{1,0:T(8,128)(2,1)S(1)}, u32[]{:S(2)}, u32[]{:S(2)}) collective-permute-start(bf16[96,768]{1,0:T(8,128)(2,1)} %get-tuple-element.9.own_ref), channel_id=1, source_target_pairs={{0,28},{4,0},{8,4},{12,8},{16,12},{20,16},{24,20},{28,24},{1,29},{... | collective-permute-start | bytes 442376 | tf_op jit(solution)/shard_map/ppermute | solution.py:232
  6.4 9.6 %copy-start.4 = (s32[2]{0:T(128)S(1)}, s32[2]{0:T(128)}, u32[]{:S(2)}) copy-start(s32[2]{0:T(128)} %pad_add_fusion.pos_ref) | copy-start | bytes 28
  6.4 9.6 %copy-start.5 = (f32[4]{0:T(128)S(1)}, f32[4]{0:T(128)}, u32[]{:S(2)}) copy-start(f32[4]{0:T(128)} %weight_ref.1) | copy-start | bytes 52
  6.4 5.6 %collective-permute-start.3 = (bf16[2,72,128]{2,1,0:T(8,128)(2,1)}, bf16[2,72,128]{2,1,0:T(8,128)(2,1)S(1)}, u32[]{:S(2)}, u32[]{:S(2)}) collective-permute-start(bf16[2,72,128]{2,1,0:T(8,128)(2,1)} %get-tuple-element.11.refs_0_), channel_id=1, source_target_pairs={{0,3},{1,0},{2,1},{3,2},{4,7},{5,4},{6,5},{7,6},{8,11},{9,8},{10,9... | collective-permute-start | bytes 110600 | tf_op jit(solution)/shard_map/ppermute | solution.py:234
  10.0 5.1 %collective-permute-start.2 = (bf16[2,72,128]{2,1,0:T(8,128)(2,1)}, bf16[2,72,128]{2,1,0:T(8,128)(2,1)S(1)}, u32[]{:S(2)}, u32[]{:S(2)}) collective-permute-start(bf16[2,72,128]{2,1,0:T(8,128)(2,1)} %get-tuple-element.11.refs_0_), channel_id=1, source_target_pairs={{0,2},{1,3},{2,0},{3,1},{4,6},{5,7},{6,4},{7,5},{8,10},{9,11},{10,... | collective-permute-start | bytes 110600 | tf_op jit(solution)/shard_map/ppermute | solution.py:234
  10.0 6.0 %collective-permute-start.1 = (bf16[2,72,128]{2,1,0:T(8,128)(2,1)}, bf16[2,72,128]{2,1,0:T(8,128)(2,1)S(1)}, u32[]{:S(2)}, u32[]{:S(2)}) collective-permute-start(bf16[2,72,128]{2,1,0:T(8,128)(2,1)} %get-tuple-element.11.refs_0_), channel_id=1, source_target_pairs={{0,1},{1,2},{2,3},{3,0},{4,5},{5,6},{6,7},{7,4},{8,9},{9,10},{10,1... | collective-permute-start | bytes 110600 | tf_op jit(solution)/shard_map/ppermute | solution.py:234
  16.0 0.9 %copy-start = (bf16[96,768]{1,0:T(8,128)(2,1)S(1)}, bf16[96,768]{1,0:T(8,128)(2,1)}, u32[]{:S(2)}) copy-start(bf16[96,768]{1,0:T(8,128)(2,1)} %get-tuple-element.9.own_ref) | copy-start | bytes 442372
  16.9 0.8 %copy-start.2 = (bf16[32,768]{1,0:T(8,128)(2,1)S(1)}, bf16[32,768]{1,0:T(8,128)(2,1)}, u32[]{:S(2)}) copy-start(bf16[32,768]{1,0:T(8,128)(2,1)} %get-tuple-element.10.rest_ref) | copy-start | bytes 147460
  17.7 0.8 %copy-start.3 = (bf16[2,72,128]{2,1,0:T(8,128)(2,1)S(1)}, bf16[2,72,128]{2,1,0:T(8,128)(2,1)}, u32[]{:S(2)}) copy-start(bf16[2,72,128]{2,1,0:T(8,128)(2,1)} %get-tuple-element.11.refs_0_) | copy-start | bytes 110596
  39.2 0.7 %copy-start.1 = (f32[64,512]{1,0:T(8,128)}, f32[64,512]{1,0:T(8,128)S(1)}, u32[]{:S(2)}) copy-start(f32[64,512]{1,0:T(8,128)S(1)} %get-tuple-element.12.here_ref) | copy-start | bytes 393220
  39.9 5.3 %collective-permute-start.4 = (f32[64,512]{1,0:T(8,128)S(1)}, f32[64,512]{1,0:T(8,128)S(1)}, u32[]{:S(2)}, u32[]{:S(2)}) collective-permute-start(f32[64,512]{1,0:T(8,128)S(1)} %get-tuple-element.13), channel_id=1, source_target_pairs={{0,4},{4,8},{8,12},{12,16},{16,20},{20,24},{24,28},{28,0},{1,5},{5... | collective-permute-start | bytes 393224 | tf_op jit(solution)/shard_map/ppermute | solution.py:257
  45.2 0.6 %copy-start.6 = (f32[64,512]{1,0:T(8,128)}, f32[64,512]{1,0:T(8,128)S(1)}, u32[]{:S(2)}) copy-start(f32[64,512]{1,0:T(8,128)S(1)} %collective-permute-done.4.came_ref) | copy-start | bytes 393220

commit v2 on v1

v2 whole, which is shorter than its diff:
```python
import functools

import jax
import jax.numpy as jnp
from jax import lax
from jax.experimental import pallas as pl
from jax.experimental.pallas import tpu as pltpu
from jax.sharding import PartitionSpec as P

POLY_DEV = 256

steepness = 8.0
threshold = 0.67

F32 = jnp.float32
BF16 = jnp.bfloat16
LANES = 128
SIDE = 64
GROUP = 16
FACTS = 7
ANY = pl.BlockSpec(memory_space=pl.ANY)
VMEM = pl.BlockSpec(memory_space=pltpu.VMEM)
SMEM = pl.BlockSpec(memory_space=pltpu.SMEM)


def split3(value):
    high = value.astype(BF16)
    rest = value - high.astype(F32)
    middle = rest.astype(BF16)
    low = (rest - middle.astype(F32)).astype(BF16)
    return high, middle, low


def split2(value):
    high = value.astype(BF16)
    return high, (value - high.astype(F32)).astype(BF16)


def pack_kernel(
    block,
    mask_hbm,
    target_hbm,
    real_hbm,
    imag_hbm,
    pixel_hbm,
    owner_hbm,
    slot_hbm,
    weight_hbm,
    out_ref,
    rest_ref,
    taps_ref,
    mask_ref,
    target_ref,
    real_ref,
    imag_ref,
    pixel_ref,
    owner_ref,
    slot_ref,
    weight_ref,
    square,
    sems,
):
    rows, width = mask_hbm.shape
    half = rows // 2
    first = lax.axis_index("kern") * block
    left = pl.multiple_of(jnp.maximum(first - LANES, 0), LANES)
    right = pl.multiple_of(jnp.minimum(first + block, width - LANES), LANES)
    middle = pl.multiple_of(first, LANES)
    copies = []

    def fetch(source, place):
        copies.append(pltpu.make_async_copy(source, place, sems.at[len(copies)]))
        copies[-1].start()

    for source, place in ((mask_hbm, mask_ref), (target_hbm, target_ref)):
        fetch(source.at[:, pl.ds(middle, block)], place.at[:, LANES : LANES + block])
        fetch(source.at[:, pl.ds(left, LANES)], place.at[:, 0:LANES])
        fetch(source.at[:, pl.ds(right, LANES)], place.at[:, LANES + block :])
    fetch(real_hbm, real_ref)
    fetch(imag_hbm, imag_ref)
    fetch(pixel_hbm, pixel_ref)
    fetch(owner_hbm, owner_ref)
    fetch(slot_hbm, slot_ref)
    fetch(weight_hbm, weight_ref)
    square[...] = jnp.zeros_like(square)
    for copy in copies:
        copy.wait()

    whole = block + 2 * SIDE
    cut = slice(LANES - SIDE, LANES - SIDE + whole)
    column = first - SIDE + lax.broadcasted_iota(jnp.int32, (rows, whole), 1)
    inside = jnp.logical_and(column >= 0, column < width)
    mask = jnp.where(inside, mask_ref[...].astype(F32)[:, cut], 0.0)
    out_ref[0:rows, :] = mask.astype(BF16)
    target = target_ref[...].astype(F32)[:, cut].astype(BF16)
    out_ref[rows : rows + half, :] = target[:half]
    rest_ref[...] = target[half:]

    pixel = pixel_ref[...]
    pixel_high = pixel // LANES
    facts = [pixel_high, pixel - pixel_high * LANES, owner_ref[...], slot_ref[...]]
    facts = [fact.astype(F32) for fact in facts] + [part.astype(F32) for part in split3(weight_ref[...])]
    beside = whole // LANES
    layers = (out_ref.shape[0] - rows - half) // facts[0].shape[0]
    facts += [jnp.zeros_like(facts[0])] * (layers * beside - len(facts))
    lines = [jnp.concatenate(facts[at * beside : (at + 1) * beside], 1) for at in range(layers)]
    out_ref[rows + half :, :] = jnp.concatenate(lines, 0).astype(BF16)

    ksize = real_ref.shape[1]
    for kernel in range(real_ref.shape[0]):
        for part, ref in enumerate((real_ref, imag_ref)):
            square[0:ksize, 0:ksize] = ref[kernel].astype(F32)
            taps_ref[2 * kernel + part] = square[...].T[: taps_ref.shape[1]].astype(BF16)


def field_kernel(block, width, ksize, n_sets, weight_ref, *refs):
    sources = refs[: 3 + n_sets]
    here_ref, there_hbm, sums_ref = refs[3 + n_sets : 6 + n_sets]
    landed = refs[6 + n_sets : 9 + 2 * n_sets]
    own_ref, next_ref, rest_ref = landed[:3]
    tap_refs = landed[3:]
    (
        there_ref,
        taps32,
        mask_t,
        target_t,
        shifted,
        band,
        tail_band,
        fields,
        products,
        parts,
        row_hits,
        slot_hits,
        sems,
        out_sem,
    ) = refs[9 + 2 * n_sets :]
    radius = (ksize - 1) // 2
    per_set = tap_refs[0].shape[0]
    pairs = n_sets * per_set // 2
    rows = here_ref.shape[0]
    half = rows // 2
    window = 2 * rows
    span = block + 2 * radius
    tall = span + 2 * radius
    tall_out = block + GROUP
    groups = (ksize - 1) // GROUP
    height = 2 * pairs * rows
    kern_at = lax.axis_index("kern")
    last = lax.axis_index("tile") == lax.axis_size("tile") - 1

    copies = [
        pltpu.make_async_copy(source, place, sems.at[at])
        for at, (source, place) in enumerate(zip(sources, landed))
    ]
    for copy in copies:
        copy.start()
    for copy in copies[3:]:
        copy.wait()
    for index, ref in enumerate(tap_refs):
        taps32[index * per_set : (index + 1) * per_set] = ref[...].astype(F32)

    out_row = lax.broadcasted_iota(jnp.int32, (rows, window), 0) < half
    in_row = lax.broadcasted_iota(jnp.int32, (rows, window), 1) < rows
    keep = jnp.logical_or(out_row == in_row, jnp.logical_not(last))
    keep = keep.astype(F32)

    def toeplitz(component, b):
        row = jnp.broadcast_to(taps32[component, b : b + 1, :], (rows, window))
        return (pltpu.roll(row, 0, 1, stride=1, stride_axis=0) * keep).astype(BF16)

    def build(group):
        for j in range(GROUP):
            for component in range(2 * pairs):
                top = group * height + component * rows
                band[top : top + rows, j * window : (j + 1) * window] = toeplitz(
                    component, group * GROUP + j
                )

    for component in range(2 * pairs):
        tail_band[component * rows : (component + 1) * rows, :] = toeplitz(component, ksize - 1)
    build(0)

    for copy in copies[:3]:
        copy.wait()
    for piece in range(mask_t.shape[0] // LANES):
        lanes = slice(piece * LANES, (piece + 1) * LANES)
        both = jnp.concatenate([own_ref[0:rows, lanes], next_ref[0:rows, lanes]], 0)
        mask_t[lanes, :] = both.astype(F32).T
        one = jnp.concatenate([rest_ref[:, lanes], next_ref[rows : rows + half, lanes]], 0)
        target_t[lanes, :] = jnp.concatenate([one, one], 0).astype(F32).T
    base = SIDE - 2 * radius
    for j in range(GROUP):
        count = tall if j == 0 else tall - GROUP
        shifted[0:count, j * window : (j + 1) * window] = mask_t[base + j : base + j + count, :].astype(BF16)

    nt = (((1,), (1,)), ((), ()))
    fields[...] = lax.dot_general(
        shifted[2 * radius :, 0:window], tail_band[...], nt, preferred_element_type=F32
    )
    for group in range(groups):
        if group + 1 < groups:
            build(group + 1)
        fields[...] += lax.dot_general(
            shifted[group * GROUP : group * GROUP + span, :],
            band[group * height : (group + 1) * height, :],
            nt,
            preferred_element_type=F32,
        )

    weights = []
    for index in range(n_sets):
        source = lax.rem(kern_at - index + n_sets, n_sets)
        for kernel in range(per_set // 2):
            weights.append(weight_ref[source * (per_set // 2) + kernel])
    total_weight = weight_ref[0]
    for kernel in range(1, pairs):
        total_weight = total_weight + weight_ref[kernel]
    total_weight = jnp.full((1, window), total_weight, F32)
    intensity = jnp.zeros((span, window), F32)
    for kernel in range(pairs):
        field = fields[:, kernel * window : (kernel + 1) * window]
        intensity = intensity + weights[kernel] * field * field
    intensity = intensity + pltpu.roll(intensity, rows, 1)
    resist = jax.nn.sigmoid(steepness * (intensity / total_weight - threshold))
    target = target_t[SIDE - radius : SIDE - radius + span, :]
    slope = 2.0 * (resist - target) * steepness * resist * (1.0 - resist) / total_weight
    column = kern_at * block - radius + lax.broadcasted_iota(jnp.int32, (span, window), 0)
    slope = jnp.where(jnp.logical_and(column >= 0, column < width), slope, 0.0)
    for kernel in range(pairs):
        lanes = slice(kernel * window, (kernel + 1) * window)
        value = ((2.0 * weights[kernel]) * slope * fields[:, lanes]).astype(BF16)
        for group in range(groups):
            skip = (groups - 1 - group) * GROUP
            left = group * height + kernel * window
            products[:, left : left + window] = value[skip : skip + tall_out]

    beside = own_ref.shape[1] // LANES
    deep = 8

    def fact(index):
        top, left = index // beside * deep, index % beside * LANES
        lines = []
        for ref in (own_ref, next_ref):
            tile = ref[rows + half :, :].astype(F32)[top : top + deep, left : left + LANES]
            lines += [tile[at : at + 1] for at in range(deep)]
        return jnp.concatenate(lines, 1)

    pixel = (fact(0) * LANES + fact(1)).astype(jnp.int32)
    owner = fact(2).astype(jnp.int32)
    slot = fact(3).astype(jnp.int32)
    edge_weight = fact(4) + fact(5) + fact(6)
    edges = pixel.shape[1]
    row = pixel // block
    col = pixel - row * block
    row = row + jnp.where(lax.broadcasted_iota(jnp.int32, (1, edges), 1) < edges // 2, 0, rows)
    row_hit = (lax.broadcasted_iota(jnp.int32, (window, edges), 0) == row).astype(F32).astype(BF16)
    row_hits[0:window, :] = row_hit
    row_hits[window:, :] = row_hit
    slots = slot_hits.shape[0]
    slot_hits[...] = (lax.broadcasted_iota(jnp.int32, (slots, edges), 0) == slot).astype(F32).astype(BF16)

    for j in range(0, GROUP, 2):
        two = jnp.dot(products[...], band[:, j * window : (j + 2) * window], preferred_element_type=F32)
        parts[j] = two[:, :window]
        parts[j + 1] = two[:, window:]
    total = jnp.dot(products[0:block, (groups - 1) * height :], tail_band[...], preferred_element_type=F32)
    for j in range(GROUP):
        total = total + parts[j, GROUP - j : GROUP - j + block, :]
    for piece in range(block // LANES):
        lanes = slice(piece * LANES, (piece + 1) * LANES)
        turned = total[piece * LANES : (piece + 1) * LANES, :].T
        here_ref[:, lanes] = turned[:rows]
        there_ref[:, lanes] = turned[rows:]
    send = pltpu.make_async_copy(there_ref, there_hbm, out_sem)
    send.start()

    both = jnp.concatenate(split2(total), 1)
    picked = jnp.dot(both, row_hits[...], preferred_element_type=F32)
    col_hit = lax.broadcasted_iota(jnp.int32, (block, edges), 0) == col
    value = jnp.sum(jnp.where(col_hit, picked, 0.0), 0, keepdims=True) * edge_weight
    tiles = sums_ref.shape[0] // n_sets
    spread = jnp.where(lax.broadcasted_iota(jnp.int32, (tiles, edges), 0) == owner, value, 0.0)
    spread = jnp.concatenate([part.astype(F32) for part in split2(spread)], 0).astype(BF16)
    sums = lax.dot_general(spread, slot_hits[...], nt, preferred_element_type=F32)
    sums = sums[:tiles] + sums[tiles:]
    for tile in range(tiles):
        sums_ref[tile * n_sets : (tile + 1) * n_sets, :] = jnp.broadcast_to(
            sums[tile : tile + 1], (n_sets, slots)
        )
    send.wait()


def on_device(
    mask_field,
    target_map,
    kernel_real,
    kernel_imag,
    socs_weight,
    edge_pixel,
    edge_owner,
    edge_slot,
    edge_weight,
):
    rows, width = mask_field.shape
    half = rows // 2
    count, ksize = kernel_real.shape[:2]
    tiles, kerns = lax.axis_size("tile"), lax.axis_size("kern")
    block = width // kerns
    radius = (ksize - 1) // 2
    span = block + 2 * radius
    whole = block + 2 * SIDE
    groups = (ksize - 1) // GROUP
    edges = edge_pixel.shape[0]
    tap_rows = -(-ksize // 8) * 8
    layers = -(-FACTS // (whole // LANES))
    layers += layers % 2
    tall = rows + half + layers * 8
    tiled = (edges // LANES, LANES)
    own, rest, taps = pl.pallas_call(
        functools.partial(pack_kernel, block),
        out_shape=(
            jax.ShapeDtypeStruct((tall, whole), BF16),
            jax.ShapeDtypeStruct((half, whole), BF16),
            jax.ShapeDtypeStruct((2 * count, tap_rows, LANES), BF16),
        ),
        in_specs=[ANY] * 8,
        out_specs=(VMEM,) * 3,
        scratch_shapes=[
            pltpu.VMEM((rows, block + 2 * LANES), BF16),
            pltpu.VMEM((rows, block + 2 * LANES), jnp.int32),
            pltpu.VMEM(kernel_real.shape, BF16),
            pltpu.VMEM(kernel_imag.shape, BF16),
            pltpu.VMEM(tiled, jnp.int32),
            pltpu.VMEM(tiled, jnp.int32),
            pltpu.VMEM(tiled, jnp.int32),
            pltpu.VMEM(tiled, F32),
            pltpu.VMEM((LANES, LANES), F32),
            pltpu.SemaphoreType.DMA((12,)),
        ],
        name="pack",
    )(
        mask_field,
        target_map,
        kernel_real,
        kernel_imag,
        edge_pixel.reshape(tiled),
        edge_owner.reshape(tiled),
        edge_slot.reshape(tiled),
        edge_weight.reshape(tiled),
    )

    following = lax.ppermute(own, "tile", [(i, (i - 1) % tiles) for i in range(tiles)])
    tap_sets = [taps] + [
        lax.ppermute(taps, "kern", [(i, (i + step) % kerns) for i in range(kerns)])
        for step in range(1, kerns)
    ]
    sources = [own, following, rest, *tap_sets]
    components = 2 * count * kerns
    height = components * rows
    here, there, sums = pl.pallas_call(
        functools.partial(field_kernel, block, width, ksize, kerns),
        out_shape=(
            jax.ShapeDtypeStruct((rows, block), F32),
            jax.ShapeDtypeStruct((rows, block), F32),
            jax.ShapeDtypeStruct((tiles * kerns, POLY_DEV), F32),
        ),
        in_specs=[SMEM] + [ANY] * len(sources),
        out_specs=(VMEM, ANY, VMEM),
        scratch_shapes=[pltpu.VMEM(source.shape, source.dtype) for source in sources]
        + [
            pltpu.VMEM((rows, block), F32),
            pltpu.VMEM((components, tap_rows, LANES), F32),
            pltpu.VMEM((whole, LANES), F32),
            pltpu.VMEM((whole, LANES), F32),
            pltpu.VMEM((span + 2 * radius, GROUP * LANES), BF16),
            pltpu.VMEM((groups * height, GROUP * LANES), BF16),
            pltpu.VMEM((height, LANES), BF16),
            pltpu.VMEM((span, height), F32),
            pltpu.VMEM((block + GROUP, groups * height), BF16),
            pltpu.VMEM((GROUP, block + GROUP, LANES), F32),
            pltpu.VMEM((2 * LANES, 2 * edges), BF16),
            pltpu.VMEM((POLY_DEV, 2 * edges), BF16),
            pltpu.SemaphoreType.DMA((len(sources),)),
            pltpu.SemaphoreType.DMA,
        ],
        compiler_params=pltpu.CompilerParams(
            vmem_limit_bytes=groups * height * GROUP * LANES * 2 + (24 << 20)
        ),
        name="fields",
    )(socs_weight, *sources)
    came = lax.ppermute(there, "tile", [(i, (i + 1) % tiles) for i in range(tiles)])
    got = lax.all_to_all(sums, ("tile", "kern"), 0, 0, tiled=True)
    return (here + came, jnp.sum(got, 0))


def solution(mesh):
    placed = (
        P("tile", None),
        P("tile", None),
        P("kern", None, None),
        P("kern", None, None),
        P(),
        P(("tile", "kern")),
        P(("tile", "kern"), None),
        P(("tile", "kern")),
        P(("tile", "kern")),
    )
    return jax.shard_map(
        on_device,
        mesh=mesh,
        in_specs=placed,
        out_specs=(P("tile", "kern"), P("tile")),
        check_vma=False,
    )
```

time: 60.2 us -> 45.7 us (0.76)
  Pallas kernels: 26.2 us -> 17.3 us
  waiting for transfers between devices: 10.2 us -> 4.96 us
  local copies, waits for them, and re-layouts: 4.51 us -> 2.49 us
  blocking collectives: 8.99 us -> 10.7 us
    pallas_call x1, Pallas kernels: 20.8 us -> 15.4 us  [on_device(): pl.pallas_call(functools.partial(field_kernel, block, width, ksize, kerns...]
    ppermute x1, waiting for transfers between devices: 5.29 us -> 0.01 us  [on_device(): lax.ppermute(there, 'tile', [(i, (i + 1) % tiles) for i in range(tiles)])]
    pallas_call x1 -> x0, Pallas kernels: 3.63 us -> none  [on_device(): pl.pallas_call(edge_kernel, out_shape=(jax.ShapeDtypeStruct((rows, block)...]
    all_to_all x1, blocking collectives: 8.99 us -> 10.7 us  [on_device(): got = lax.all_to_all(sums, ('tile', 'kern'), 0, 0, tiled=True)]
    unnamed x14 -> x8, local copies, waits for them, and re-layouts: 3.77 us -> 2.46 us
    broadcast_in_dim x1 -> x0, local copies, waits for them, and re-layouts: 0.7 us -> none  [on_device(): spread = jnp.repeat(sums, kerns, axis=0)]
    add x0 -> x1, other arithmetic: none -> 0.67 us  [on_device(): return (here + came, jnp.sum(got, 0))]
  transfers between devices with their start and end apart: 5 -> 5, of which waited for: 4 -> 3; matrix products, arithmetic and copies ran while one was open for 0% -> 1% of each run, Pallas kernels for 0% -> 0%
where the time goes in v2:
time: 45.7 us; the launch traced here: 45.4 us
  Pallas kernels  17.3 us (38%)
  blocking collectives  10.7 us (23%)
  starting transfers between devices  8.06 us (18%)
  waiting for transfers between devices  4.96 us (11%)
  local copies, waits for them, and re-layouts  2.49 us (5%)
  other arithmetic  1.29 us (3%)
  between operations  0.68 us (1%)
    pallas_call x1, Pallas kernels, on_device(): pl.pallas_call(functools.partial(field_kernel, block, width, ksize, kerns...  15.4 us
    all_to_all x1, blocking collectives, on_device(): got = lax.all_to_all(sums, ('tile', 'kern'), 0, 0, tiled=True)  10.7 us
    ppermute x3, waiting for transfers between devices, on_device(): lax.ppermute(taps, 'kern', [(i, (i + step) % kerns) for i in range(kerns)])  4.95 us
    ppermute x3, starting transfers between devices, on_device(): lax.ppermute(taps, 'kern', [(i, (i + step) % kerns) for i in range(kerns)])  4.62 us
    ppermute x1, starting transfers between devices, on_device(): lax.ppermute(own, 'tile', [(i, (i - 1) % tiles) for i in range(tiles)])  3.39 us
    unnamed x8, local copies, waits for them, and re-layouts  2.46 us
    pallas_call x1, Pallas kernels, on_device(): pl.pallas_call(functools.partial(pack_kernel, block), out_shape=(jax.Shap...  1.89 us
  transfers between devices with their start and end apart: 5, of which 3 were waited for; matrix products, arithmetic and copies ran while one was open for 1% of the time, Pallas kernels for 0%

profile of v2, /device:TPU:0, one launch (start us, length us, event | category | flops | bytes accessed | tf_op | source)
XLA Modules:
  0.0 45.4 jit_solution(4702846244273024976)
XLA Ops:
  0.6 1.9 %pack.1 = (bf16[112,640]{1,0:T(8,128)(2,1)}, bf16[32,640]{1,0:T(8,128)(2,1)}, bf16[2,72,128]{2,1,0:T(8,128)(2,1)}) custom-call(bf16[64,2048]{1,0:T(8,128)(2,1)} %mask_hbm.1, s32[64,2048]{1,0:T(8,128)} %target_hbm.1, bf16[1,65,65]{2,1,0:T(8,128)(2,1)} %real_hbm.1, bf16[1,65,65]{2,1,0:T(8,128)(2,1)} %imag_hbm.1, s32[8,128]{1,0:T(8,128)} %bitcast.6, ...), custom_call_target="tpu_custom_call" | custom-call | tf_op jit(solution)/shard_map/pack/pallas_call | solution.py:320
  2.5 3.4 %collective-permute-start = (bf16[112,640]{1,0:T(8,128)(2,1)}, bf16[112,640]{1,0:T(8,128)(2,1)S(1)}, u32[]{:S(2)}, u32[]{:S(2)}) collective-permute-start(bf16[112,640]{1,0:T(8,128)(2,1)} %get-tuple-element.8.refs_0_), channel_id=1, source_target_pairs={{0,28},{4,0},{8,4},{12,8},{16,12},{20,16},{24,20},{28,24},{1,29},{... | collective-permute-start | bytes 430088 | tf_op jit(solution)/shard_map/ppermute | solution.py:353
  5.9 0.0 copy-start.3
  5.9 3.6 %collective-permute-start.3 = (bf16[2,72,128]{2,1,0:T(8,128)(2,1)}, bf16[2,72,128]{2,1,0:T(8,128)(2,1)S(1)}, u32[]{:S(2)}, u32[]{:S(2)}) collective-permute-start(bf16[2,72,128]{2,1,0:T(8,128)(2,1)} %get-tuple-element.10.refs_3_), channel_id=1, source_target_pairs={{0,3},{1,0},{2,1},{3,2},{4,7},{5,4},{6,5},{7,6},{8,11},{9,8},{10,9... | collective-permute-start | bytes 110600 | tf_op jit(solution)/shard_map/ppermute | solution.py:355
  9.5 0.0 collective-permute-start.2
  9.5 1.0 %collective-permute-start.1 = (bf16[2,72,128]{2,1,0:T(8,128)(2,1)}, bf16[2,72,128]{2,1,0:T(8,128)(2,1)S(1)}, u32[]{:S(2)}, u32[]{:S(2)}) collective-permute-start(bf16[2,72,128]{2,1,0:T(8,128)(2,1)} %get-tuple-element.10.refs_3_), channel_id=1, source_target_pairs={{0,1},{1,2},{2,3},{3,0},{4,5},{5,6},{6,7},{7,4},{8,9},{9,10},{10,1... | collective-permute-start | bytes 110600 | tf_op jit(solution)/shard_map/ppermute | solution.py:355
  10.5 0.9 %collective-permute-done.3.refs_6_ = bf16[2,72,128]{2,1,0:T(8,128)(2,1)S(1)} collective-permute-done((bf16[2,72,128]{2,1,0:T(8,128)(2,1)}, bf16[2,72,128]{2,1,0:T(8,128)(2,1)S(1)}, u32[]{:S(2)}, u32[]{:S(2)}) %collective-permute-start.3) | collective-permute-done | bytes 36896 | tf_op jit(solution)/shard_map/ppermute | solution.py:355
  11.5 3.1 %collective-permute-done.2.refs_5_ = bf16[2,72,128]{2,1,0:T(8,128)(2,1)S(1)} collective-permute-done((bf16[2,72,128]{2,1,0:T(8,128)(2,1)}, bf16[2,72,128]{2,1,0:T(8,128)(2,1)S(1)}, u32[]{:S(2)}, u32[]{:S(2)}) %collective-permute-start.2) | collective-permute-done | bytes 36896 | tf_op jit(solution)/shard_map/ppermute | solution.py:355
  14.6 0.9 %collective-permute-done.1.refs_4_ = bf16[2,72,128]{2,1,0:T(8,128)(2,1)S(1)} collective-permute-done((bf16[2,72,128]{2,1,0:T(8,128)(2,1)}, bf16[2,72,128]{2,1,0:T(8,128)(2,1)S(1)}, u32[]{:S(2)}, u32[]{:S(2)}) %collective-permute-start.1) | collective-permute-done | bytes 36896 | tf_op jit(solution)/shard_map/ppermute | solution.py:355
  15.5 0.0 collective-permute-done.refs_1_
  15.5 0.0 copy-done.3
  15.5 0.0 copy-start
  15.5 0.9 %copy-done = bf16[112,640]{1,0:T(8,128)(2,1)S(1)} copy-done((bf16[112,640]{1,0:T(8,128)(2,1)S(1)}, bf16[112,640]{1,0:T(8,128)(2,1)}, u32[]{:S(2)}) %copy-start) | copy-done | bytes 143384
  16.4 0.0 copy-start.1
  16.4 0.8 %copy-done.1 = bf16[32,640]{1,0:T(8,128)(2,1)S(1)} copy-done((bf16[32,640]{1,0:T(8,128)(2,1)S(1)}, bf16[32,640]{1,0:T(8,128)(2,1)}, u32[]{:S(2)}) %copy-start.1) | copy-done | bytes 40984
  17.2 0.0 copy-start.2
  17.2 0.8 %copy-done.2 = bf16[2,72,128]{2,1,0:T(8,128)(2,1)S(1)} copy-done((bf16[2,72,128]{2,1,0:T(8,128)(2,1)S(1)}, bf16[2,72,128]{2,1,0:T(8,128)(2,1)}, u32[]{:S(2)}) %copy-start.2) | copy-done | bytes 36888
  18.0 15.4 %fields.1 = (f32[64,512]{1,0:T(8,128)S(1)}, f32[64,512]{1,0:T(8,128)S(1)}, f32[32,256]{1,0:T(8,128)S(1)}) custom-call(f32[4]{0:T(128)S(1)} %copy-done.3, bf16[112,640]{1,0:T(8,128)(2,1)S(1)} %copy-done, bf16[112,640]{1,0:T(8,128)(2,1)S(1)} %collective-permute-done.refs_1_, bf16[32,640]{1,0:T(8,128)(2,1)S(1)} %copy-done.1, bf16[2,72,128]{2,1,0:T(8,128)(2,1)S(1)} %copy-done.2, ...), custom_call_target="tpu_custom_call" | custom-call | tf_op jit(solution)/shard_map/fields/pallas_call | solution.py:361
  33.3 0.1 collective-permute-start.4
  33.4 10.7 %all_to_all.9 = f32[32,1,256]{2,1,0:T(1,128)S(1)} all-to-all(f32[32,1,256]{2,1,0:T(1,128)S(1)} %copy.11), channel_id=1, replica_groups=mesh['tile'=8,'kern'=4] {'tile','kern'}, dimensions={0} | all-to-all | bytes 65536 | tf_op jit(solution)/shard_map/all_to_all | solution.py:393
  44.1 0.6 %reduce_sum.9 = f32[256]{0:T(256)} reduce(f32[32,1,256]{2,1,0:T(1,128)S(1)} %all_to_all.9, f32[]{:T(128)} %constant.0.clone.1), dimensions={0,1}, to_apply=%region_0.0 | reduce | flops 7936 | bytes 33796 | tf_op jit(solution)/shard_map/reduce_sum | solution.py:394
  44.7 0.0 collective-permute-done.4
  44.7 0.7 %add.3 = f32[64,512]{1,0:T(8,128)} add(f32[64,512]{1,0:T(8,128)S(1)} %get-tuple-element.11, f32[64,512]{1,0:T(8,128)S(1)} %collective-permute-done.4) | non-fusion elementwise | flops 32768 | bytes 393216 | tf_op jit(solution)/shard_map/add | solution.py:394
  (1 shorter events, 0.0 us)
Async XLA Ops:
  2.5 13.0 %collective-permute-start = (bf16[112,640]{1,0:T(8,128)(2,1)}, bf16[112,640]{1,0:T(8,128)(2,1)S(1)}, u32[]{:S(2)}, u32[]{:S(2)}) collective-permute-start(bf16[112,640]{1,0:T(8,128)(2,1)} %get-tuple-element.8.refs_0_), channel_id=1, source_target_pairs={{0,28},{4,0},{8,4},{12,8},{16,12},{20,16},{24,20},{28,24},{1,29},{... | collective-permute-start | bytes 430088 | tf_op jit(solution)/shard_map/ppermute | solution.py:353
  5.9 9.6 %copy-start.3 = (f32[4]{0:T(128)S(1)}, f32[4]{0:T(128)}, u32[]{:S(2)}) copy-start(f32[4]{0:T(128)} %weight_ref.1) | copy-start | bytes 52
  5.9 5.6 %collective-permute-start.3 = (bf16[2,72,128]{2,1,0:T(8,128)(2,1)}, bf16[2,72,128]{2,1,0:T(8,128)(2,1)S(1)}, u32[]{:S(2)}, u32[]{:S(2)}) collective-permute-start(bf16[2,72,128]{2,1,0:T(8,128)(2,1)} %get-tuple-element.10.refs_3_), channel_id=1, source_target_pairs={{0,3},{1,0},{2,1},{3,2},{4,7},{5,4},{6,5},{7,6},{8,11},{9,8},{10,9... | collective-permute-start | bytes 110600 | tf_op jit(solution)/shard_map/ppermute | solution.py:355
  9.5 5.1 %collective-permute-start.2 = (bf16[2,72,128]{2,1,0:T(8,128)(2,1)}, bf16[2,72,128]{2,1,0:T(8,128)(2,1)S(1)}, u32[]{:S(2)}, u32[]{:S(2)}) collective-permute-start(bf16[2,72,128]{2,1,0:T(8,128)(2,1)} %get-tuple-element.10.refs_3_), channel_id=1, source_target_pairs={{0,2},{1,3},{2,0},{3,1},{4,6},{5,7},{6,4},{7,5},{8,10},{9,11},{10,... | collective-permute-start | bytes 110600 | tf_op jit(solution)/shard_map/ppermute | solution.py:355
  9.5 6.0 %collective-permute-start.1 = (bf16[2,72,128]{2,1,0:T(8,128)(2,1)}, bf16[2,72,128]{2,1,0:T(8,128)(2,1)S(1)}, u32[]{:S(2)}, u32[]{:S(2)}) collective-permute-start(bf16[2,72,128]{2,1,0:T(8,128)(2,1)} %get-tuple-element.10.refs_3_), channel_id=1, source_target_pairs={{0,1},{1,2},{2,3},{3,0},{4,5},{5,6},{6,7},{7,4},{8,9},{9,10},{10,1... | collective-permute-start | bytes 110600 | tf_op jit(solution)/shard_map/ppermute | solution.py:355
  15.5 0.9 %copy-start = (bf16[112,640]{1,0:T(8,128)(2,1)S(1)}, bf16[112,640]{1,0:T(8,128)(2,1)}, u32[]{:S(2)}) copy-start(bf16[112,640]{1,0:T(8,128)(2,1)} %get-tuple-element.8.refs_0_) | copy-start | bytes 430084
  16.4 0.8 %copy-start.1 = (bf16[32,640]{1,0:T(8,128)(2,1)S(1)}, bf16[32,640]{1,0:T(8,128)(2,1)}, u32[]{:S(2)}) copy-start(bf16[32,640]{1,0:T(8,128)(2,1)} %get-tuple-element.9.refs_2_) | copy-start | bytes 122884
  17.2 0.8 %copy-start.2 = (bf16[2,72,128]{2,1,0:T(8,128)(2,1)S(1)}, bf16[2,72,128]{2,1,0:T(8,128)(2,1)}, u32[]{:S(2)}) copy-start(bf16[2,72,128]{2,1,0:T(8,128)(2,1)} %get-tuple-element.10.refs_3_) | copy-start | bytes 110596
  33.3 11.4 %collective-permute-start.4 = (f32[64,512]{1,0:T(8,128)S(1)}, f32[64,512]{1,0:T(8,128)S(1)}, u32[]{:S(2)}, u32[]{:S(2)}) collective-permute-start(f32[64,512]{1,0:T(8,128)S(1)} %get-tuple-element.12), channel_id=1, source_target_pairs={{0,4},{4,8},{8,12},{12,16},{16,20},{20,24},{24,28},{28,0},{1,5},{5... | collective-permute-start | bytes 393224 | tf_op jit(solution)/shard_map/ppermute | solution.py:392

commit v3 on v2

--- a/solution.py
+++ b/solution.py
@@ -18,7 +18,7 @@
 SIDE = 64
 GROUP = 16
 FACTS = 7
-ANY = pl.BlockSpec(memory_space=pl.ANY)
+HBM = pl.BlockSpec(memory_space=pltpu.HBM)
 VMEM = pl.BlockSpec(memory_space=pltpu.VMEM)
 SMEM = pl.BlockSpec(memory_space=pltpu.SMEM)
 
@@ -130,7 +130,8 @@
         fields,
         products,
         parts,
-        row_hits,
+        total_ref,
+        spot_hits,
         slot_hits,
         sems,
         out_sem,
@@ -169,9 +170,9 @@
         row = jnp.broadcast_to(taps32[component, b : b + 1, :], (rows, window))
         return (pltpu.roll(row, 0, 1, stride=1, stride_axis=0) * keep).astype(BF16)
 
-    def build(group):
+    def build(group, side):
         for j in range(GROUP):
-            for component in range(2 * pairs):
+            for component in range(side * pairs, (side + 1) * pairs):
                 top = group * height + component * rows
                 band[top : top + rows, j * window : (j + 1) * window] = toeplitz(
                     component, group * GROUP + j
@@ -179,7 +180,7 @@
 
     for component in range(2 * pairs):
         tail_band[component * rows : (component + 1) * rows, :] = toeplitz(component, ksize - 1)
-    build(0)
+    build(0, 0)
 
     for copy in copies[:3]:
         copy.wait()
@@ -198,12 +199,14 @@
     fields[...] = lax.dot_general(
         shifted[2 * radius :, 0:window], tail_band[...], nt, preferred_element_type=F32
     )
-    for group in range(groups):
-        if group + 1 < groups:
-            build(group + 1)
-        fields[...] += lax.dot_general(
+    steps = [(group, side) for group in range(groups) for side in range(2)]
+    part = height // 2
+    for at, (group, side) in enumerate(steps):
+        if at + 1 < len(steps):
+            build(*steps[at + 1])
+        fields[:, side * part : (side + 1) * part] += lax.dot_general(
             shifted[group * GROUP : group * GROUP + span, :],
-            band[group * height : (group + 1) * height, :],
+            band[group * height + side * part : group * height + (side + 1) * part, :],
             nt,
             preferred_element_type=F32,
         )
@@ -253,31 +256,43 @@
     edges = pixel.shape[1]
     row = pixel // block
     col = pixel - row * block
+    piece = col // LANES
+    col = col - piece * LANES
     row = row + jnp.where(lax.broadcasted_iota(jnp.int32, (1, edges), 1) < edges // 2, 0, rows)
-    row_hit = (lax.broadcasted_iota(jnp.int32, (window, edges), 0) == row).astype(F32).astype(BF16)
-    row_hits[0:window, :] = row_hit
-    row_hits[window:, :] = row_hit
+    pieces = block // LANES
+    spot = piece * window + row
+    spot_hits[...] = (
+        (lax.broadcasted_iota(jnp.int32, (pieces * window, edges), 0) == spot).astype(F32).astype(BF16)
+    )
     slots = slot_hits.shape[0]
     slot_hits[...] = (lax.broadcasted_iota(jnp.int32, (slots, edges), 0) == slot).astype(F32).astype(BF16)
 
+    def moved(j):
+        return parts[j, GROUP - j : GROUP - j + block, :]
+
+    total_ref[...] = jnp.dot(
+        products[0:block, (groups - 1) * height :], tail_band[...], preferred_element_type=F32
+    )
     for j in range(0, GROUP, 2):
         two = jnp.dot(products[...], band[:, j * window : (j + 2) * window], preferred_element_type=F32)
         parts[j] = two[:, :window]
         parts[j + 1] = two[:, window:]
-    total = jnp.dot(products[0:block, (groups - 1) * height :], tail_band[...], preferred_element_type=F32)
-    for j in range(GROUP):
-        total = total + parts[j, GROUP - j : GROUP - j + block, :]
-    for piece in range(block // LANES):
+        if j >= 2:
+            total_ref[...] += moved(j - 2) + moved(j - 1)
+    total = total_ref[...] + moved(GROUP - 2) + moved(GROUP - 1)
+    tiles_of_total = [total[piece * LANES : (piece + 1) * LANES, :] for piece in range(pieces)]
+    for piece in range(pieces):
         lanes = slice(piece * LANES, (piece + 1) * LANES)
-        turned = total[piece * LANES : (piece + 1) * LANES, :].T
+        turned = tiles_of_total[piece].T
         here_ref[:, lanes] = turned[:rows]
         there_ref[:, lanes] = turned[rows:]
     send = pltpu.make_async_copy(there_ref, there_hbm, out_sem)
     send.start()
 
-    both = jnp.concatenate(split2(total), 1)
-    picked = jnp.dot(both, row_hits[...], preferred_element_type=F32)
-    col_hit = lax.broadcasted_iota(jnp.int32, (block, edges), 0) == col
+    two = jnp.concatenate(split2(jnp.concatenate(tiles_of_total, 1)), 0)
+    picked = jnp.dot(two, spot_hits[...], preferred_element_type=F32)
+    picked = picked[:LANES] + picked[LANES:]
+    col_hit = lax.broadcasted_iota(jnp.int32, (LANES, edges), 0) == col
     value = jnp.sum(jnp.where(col_hit, picked, 0.0), 0, keepdims=True) * edge_weight
     tiles = sums_ref.shape[0] // n_sets
     spread = jnp.where(lax.broadcasted_iota(jnp.int32, (tiles, edges), 0) == owner, value, 0.0)
@@ -289,6 +304,19 @@
             sums[tile : tile + 1], (n_sets, slots)
         )
     send.wait()
+
+
+def finish_kernel(here_hbm, came_hbm, got_hbm, grad_ref, sums_ref, here_ref, came_ref, got_ref, sems):
+    copies = [
+        pltpu.make_async_copy(source, place, sems.at[at])
+        for at, (source, place) in enumerate(((here_hbm, here_ref), (came_hbm, came_ref), (got_hbm, got_ref)))
+    ]
+    for copy in copies:
+        copy.start()
+    for copy in copies:
+        copy.wait()
+    grad_ref[...] = here_ref[...] + came_ref[...]
+    sums_ref[...] = jnp.sum(got_ref[...], 0, keepdims=True)
 
 
 def on_device(
@@ -324,7 +352,7 @@
             jax.ShapeDtypeStruct((half, whole), BF16),
             jax.ShapeDtypeStruct((2 * count, tap_rows, LANES), BF16),
         ),
-        in_specs=[ANY] * 8,
+        in_specs=[HBM] * 8,
         out_specs=(VMEM,) * 3,
         scratch_shapes=[
             pltpu.VMEM((rows, block + 2 * LANES), BF16),
@@ -365,8 +393,8 @@
             jax.ShapeDtypeStruct((rows, block), F32),
             jax.ShapeDtypeStruct((tiles * kerns, POLY_DEV), F32),
         ),
-        in_specs=[SMEM] + [ANY] * len(sources),
-        out_specs=(VMEM, ANY, VMEM),
+        in_specs=[SMEM] + [HBM] * len(sources),
+        out_specs=(VMEM, HBM, VMEM),
         scratch_shapes=[pltpu.VMEM(source.shape, source.dtype) for source in sources]
         + [
             pltpu.VMEM((rows, block), F32),
@@ -379,7 +407,8 @@
             pltpu.VMEM((span, height), F32),
             pltpu.VMEM((block + GROUP, groups * height), BF16),
             pltpu.VMEM((GROUP, block + GROUP, LANES), F32),
-            pltpu.VMEM((2 * LANES, 2 * edges), BF16),
+            pltpu.VMEM((block, LANES), F32),
+            pltpu.VMEM((block, 2 * edges), BF16),
             pltpu.VMEM((POLY_DEV, 2 * edges), BF16),
             pltpu.SemaphoreType.DMA((len(sources),)),
             pltpu.SemaphoreType.DMA,
@@ -391,7 +420,23 @@
     )(socs_weight, *sources)
     came = lax.ppermute(there, "tile", [(i, (i + 1) % tiles) for i in range(tiles)])
     got = lax.all_to_all(sums, ("tile", "kern"), 0, 0, tiled=True)
-    return (here + came, jnp.sum(got, 0))
+    mask_grad, sums = pl.pallas_call(
+        finish_kernel,
+        out_shape=(
+            jax.ShapeDtypeStruct((rows, block), F32),
+            jax.ShapeDtypeStruct((1, POLY_DEV), F32),
+        ),
+        in_specs=[HBM] * 3,
+        out_specs=(VMEM,) * 2,
+        scratch_shapes=[
+            pltpu.VMEM((rows, block), F32),
+            pltpu.VMEM((rows, block), F32),
+            pltpu.VMEM(got.shape, F32),
+            pltpu.SemaphoreType.DMA((3,)),
+        ],
+        name="finish",
+    )(here, came, got)
+    return (mask_grad, sums.reshape(-1))
 
 
 def solution(mesh):

time: 45.7 us -> 47.7 us (1.044)
  local copies, waits for them, and re-layouts: 2.49 us -> 4.38 us
  Pallas kernels: 17.3 us -> 18.7 us
  other arithmetic: 1.29 us -> 0 us
    unnamed x8 -> x13, local copies, waits for them, and re-layouts: 2.46 us -> 4.35 us
    pallas_call x0 -> x1, Pallas kernels: none -> 1.66 us  [on_device(): pl.pallas_call(finish_kernel, out_shape=(jax.ShapeDtypeStruct((rows, bloc...]
    add x1 -> x0, other arithmetic: 0.67 us -> none  [on_device(): return (here + came, jnp.sum(got, 0))]
    reduce_sum x1 -> x0, other arithmetic: 0.62 us -> none  [on_device(): return (here + came, jnp.sum(got, 0))]
where the time goes in v3:
time: 47.7 us; the launch traced here: 47.4 us
  Pallas kernels  18.7 us (39%)
  blocking collectives  10.7 us (22%)
  starting transfers between devices  8 us (17%)
  waiting for transfers between devices  4.96 us (10%)
  local copies, waits for them, and re-layouts  4.38 us (9%)
  between operations  0.67 us (1%)
    pallas_call x1, Pallas kernels, on_device(): pl.pallas_call(functools.partial(field_kernel, block, width, ksize, kerns...  15.1 us
    all_to_all x1, blocking collectives, on_device(): got = lax.all_to_all(sums, ('tile', 'kern'), 0, 0, tiled=True)  10.7 us
    ppermute x3, waiting for transfers between devices, on_device(): lax.ppermute(taps, 'kern', [(i, (i + step) % kerns) for i in range(kerns)])  4.95 us
    ppermute x3, starting transfers between devices, on_device(): lax.ppermute(taps, 'kern', [(i, (i + step) % kerns) for i in range(kerns)])  4.62 us
    unnamed x13, local copies, waits for them, and re-layouts  4.35 us
    ppermute x1, starting transfers between devices, on_device(): lax.ppermute(own, 'tile', [(i, (i - 1) % tiles) for i in range(tiles)])  3.39 us
    pallas_call x1, Pallas kernels, on_device(): pl.pallas_call(functools.partial(pack_kernel, block), out_shape=(jax.Shap...  1.88 us
    pallas_call x1, Pallas kernels, on_device(): pl.pallas_call(finish_kernel, out_shape=(jax.ShapeDtypeStruct((rows, bloc...  1.66 us
  transfers between devices with their start and end apart: 5, of which 3 were waited for; matrix products, arithmetic and copies ran while one was open for 1% of the time, Pallas kernels for 0%

profile of v3, /device:TPU:0, one launch (start us, length us, event | category | flops | bytes accessed | tf_op | source)
XLA Modules:
  0.0 47.4 jit_solution(11093245126226392234)
XLA Ops:
  0.6 1.9 %pack.1 = (bf16[112,640]{1,0:T(8,128)(2,1)}, bf16[32,640]{1,0:T(8,128)(2,1)}, bf16[2,72,128]{2,1,0:T(8,128)(2,1)}) custom-call(bf16[64,2048]{1,0:T(8,128)(2,1)} %mask_hbm.1, s32[64,2048]{1,0:T(8,128)} %target_hbm.1, bf16[1,65,65]{2,1,0:T(8,128)(2,1)} %real_hbm.1, bf16[1,65,65]{2,1,0:T(8,128)(2,1)} %imag_hbm.1, s32[8,128]{1,0:T(8,128)} %bitcast.11, ...), custom_call_target="tpu_custom_call" | custom-call | tf_op jit(solution)/shard_map/pack/pallas_call | solution.py:348
  2.5 3.4 %collective-permute-start = (bf16[112,640]{1,0:T(8,128)(2,1)}, bf16[112,640]{1,0:T(8,128)(2,1)S(1)}, u32[]{:S(2)}, u32[]{:S(2)}) collective-permute-start(bf16[112,640]{1,0:T(8,128)(2,1)} %get-tuple-element.10.refs_0_), channel_id=1, source_target_pairs={{0,28},{4,0},{8,4},{12,8},{16,12},{20,16},{24,20},{28,24},{1,29},{... | collective-permute-start | bytes 430088 | tf_op jit(solution)/shard_map/ppermute | solution.py:381
  5.9 3.6 %collective-permute-start.3 = (bf16[2,72,128]{2,1,0:T(8,128)(2,1)}, bf16[2,72,128]{2,1,0:T(8,128)(2,1)S(1)}, u32[]{:S(2)}, u32[]{:S(2)}) collective-permute-start(bf16[2,72,128]{2,1,0:T(8,128)(2,1)} %get-tuple-element.12.refs_3_), channel_id=1, source_target_pairs={{0,3},{1,0},{2,1},{3,2},{4,7},{5,4},{6,5},{7,6},{8,11},{9,8},{10,9... | collective-permute-start | bytes 110600 | tf_op jit(solution)/shard_map/ppermute | solution.py:383
  9.5 0.0 collective-permute-start.2
  9.5 1.0 %collective-permute-start.1 = (bf16[2,72,128]{2,1,0:T(8,128)(2,1)}, bf16[2,72,128]{2,1,0:T(8,128)(2,1)S(1)}, u32[]{:S(2)}, u32[]{:S(2)}) collective-permute-start(bf16[2,72,128]{2,1,0:T(8,128)(2,1)} %get-tuple-element.12.refs_3_), channel_id=1, source_target_pairs={{0,1},{1,2},{2,3},{3,0},{4,5},{5,6},{6,7},{7,4},{8,9},{9,10},{10,1... | collective-permute-start | bytes 110600 | tf_op jit(solution)/shard_map/ppermute | solution.py:383
  10.5 0.9 %collective-permute-done.3.refs_6_ = bf16[2,72,128]{2,1,0:T(8,128)(2,1)S(1)} collective-permute-done((bf16[2,72,128]{2,1,0:T(8,128)(2,1)}, bf16[2,72,128]{2,1,0:T(8,128)(2,1)S(1)}, u32[]{:S(2)}, u32[]{:S(2)}) %collective-permute-start.3) | collective-permute-done | bytes 36896 | tf_op jit(solution)/shard_map/ppermute | solution.py:383
  11.5 3.1 %collective-permute-done.2.refs_5_ = bf16[2,72,128]{2,1,0:T(8,128)(2,1)S(1)} collective-permute-done((bf16[2,72,128]{2,1,0:T(8,128)(2,1)}, bf16[2,72,128]{2,1,0:T(8,128)(2,1)S(1)}, u32[]{:S(2)}, u32[]{:S(2)}) %collective-permute-start.2) | collective-permute-done | bytes 36896 | tf_op jit(solution)/shard_map/ppermute | solution.py:383
  14.6 0.9 %collective-permute-done.1.refs_4_ = bf16[2,72,128]{2,1,0:T(8,128)(2,1)S(1)} collective-permute-done((bf16[2,72,128]{2,1,0:T(8,128)(2,1)}, bf16[2,72,128]{2,1,0:T(8,128)(2,1)S(1)}, u32[]{:S(2)}, u32[]{:S(2)}) %collective-permute-start.1) | collective-permute-done | bytes 36896 | tf_op jit(solution)/shard_map/ppermute | solution.py:383
  15.5 0.0 collective-permute-done.refs_1_
  15.5 0.0 copy-done.4
  15.5 0.0 copy-start
  15.5 0.9 %copy-done = bf16[112,640]{1,0:T(8,128)(2,1)S(1)} copy-done((bf16[112,640]{1,0:T(8,128)(2,1)S(1)}, bf16[112,640]{1,0:T(8,128)(2,1)}, u32[]{:S(2)}) %copy-start) | copy-done | bytes 143384
  16.4 0.0 copy-start.2
  16.4 0.8 %copy-done.2 = bf16[32,640]{1,0:T(8,128)(2,1)S(1)} copy-done((bf16[32,640]{1,0:T(8,128)(2,1)S(1)}, bf16[32,640]{1,0:T(8,128)(2,1)}, u32[]{:S(2)}) %copy-start.2) | copy-done | bytes 40984
  17.2 0.8 %copy-done.3 = bf16[2,72,128]{2,1,0:T(8,128)(2,1)S(1)} copy-done((bf16[2,72,128]{2,1,0:T(8,128)(2,1)S(1)}, bf16[2,72,128]{2,1,0:T(8,128)(2,1)}, u32[]{:S(2)}) %copy-start.3) | copy-done | bytes 36888
  17.9 15.1 %fields.1 = (f32[64,512]{1,0:T(8,128)S(1)}, f32[64,512]{1,0:T(8,128)S(1)}, f32[32,256]{1,0:T(8,128)S(1)}) custom-call(f32[4]{0:T(128)S(1)} %copy-done.4, bf16[112,640]{1,0:T(8,128)(2,1)S(1)} %copy-done, bf16[112,640]{1,0:T(8,128)(2,1)S(1)} %collective-permute-done.refs_1_, bf16[32,640]{1,0:T(8,128)(2,1)S(1)} %copy-done.2, bf16[2,72,128]{2,1,0:T(8,128)(2,1)S(1)} %copy-done.3, ...), custom_call_target="tpu_custom_call" | custom-call | tf_op jit(solution)/shard_map/fields/pallas_call | solution.py:389
  33.1 0.0 copy-start.1
  33.1 0.6 %copy-done.1 = f32[64,512]{1,0:T(8,128)} copy-done((f32[64,512]{1,0:T(8,128)}, f32[64,512]{1,0:T(8,128)S(1)}, u32[]{:S(2)}) %copy-start.1) | copy-done | bytes 131096
  33.8 0.0 collective-permute-start.4
  33.8 10.7 %all_to_all.11 = f32[32,1,256]{2,1,0:T(1,128)S(1)} all-to-all(f32[32,1,256]{2,1,0:T(1,128)S(1)} %copy.11), channel_id=1, replica_groups=mesh['tile'=8,'kern'=4] {'tile','kern'}, dimensions={0} | all-to-all | bytes 65536 | tf_op jit(solution)/shard_map/all_to_all | solution.py:422
  44.5 0.6 %copy.14 = f32[32,1,256]{2,0,1:T(8,128)} copy(f32[32,1,256]{2,1,0:T(1,128)S(1)} %all_to_all.11) | data formatting | bytes 65536
  45.1 0.0 collective-permute-done.4.came_hbm
  45.1 0.6 %copy-done.5 = f32[64,512]{1,0:T(8,128)} copy-done((f32[64,512]{1,0:T(8,128)}, f32[64,512]{1,0:T(8,128)S(1)}, u32[]{:S(2)}) %copy-start.5) | copy-done | bytes 131096
  45.7 1.7 %finish.1 = (f32[64,512]{1,0:T(8,128)}, f32[1,256]{1,0:T(1,128)}) custom-call(f32[64,512]{1,0:T(8,128)} %copy-done.1, f32[64,512]{1,0:T(8,128)} %copy-done.5, f32[32,256]{1,0:T(8,128)} %bitcast.10), custom_call_target="tpu_custom_call" | custom-call | tf_op jit(solution)/shard_map/finish/pallas_call | solution.py:423
  (4 shorter events, 0.0 us)
Async XLA Ops:
  2.5 13.0 %collective-permute-start = (bf16[112,640]{1,0:T(8,128)(2,1)}, bf16[112,640]{1,0:T(8,128)(2,1)S(1)}, u32[]{:S(2)}, u32[]{:S(2)}) collective-permute-start(bf16[112,640]{1,0:T(8,128)(2,1)} %get-tuple-element.10.refs_0_), channel_id=1, source_target_pairs={{0,28},{4,0},{8,4},{12,8},{16,12},{20,16},{24,20},{28,24},{1,29},{... | collective-permute-start | bytes 430088 | tf_op jit(solution)/shard_map/ppermute | solution.py:381
  5.9 9.6 %copy-start.4 = (f32[4]{0:T(128)S(1)}, f32[4]{0:T(128)}, u32[]{:S(2)}) copy-start(f32[4]{0:T(128)} %weight_ref.1) | copy-start | bytes 52
  5.9 5.6 %collective-permute-start.3 = (bf16[2,72,128]{2,1,0:T(8,128)(2,1)}, bf16[2,72,128]{2,1,0:T(8,128)(2,1)S(1)}, u32[]{:S(2)}, u32[]{:S(2)}) collective-permute-start(bf16[2,72,128]{2,1,0:T(8,128)(2,1)} %get-tuple-element.12.refs_3_), channel_id=1, source_target_pairs={{0,3},{1,0},{2,1},{3,2},{4,7},{5,4},{6,5},{7,6},{8,11},{9,8},{10,9... | collective-permute-start | bytes 110600 | tf_op jit(solution)/shard_map/ppermute | solution.py:383
  9.5 5.1 %collective-permute-start.2 = (bf16[2,72,128]{2,1,0:T(8,128)(2,1)}, bf16[2,72,128]{2,1,0:T(8,128)(2,1)S(1)}, u32[]{:S(2)}, u32[]{:S(2)}) collective-permute-start(bf16[2,72,128]{2,1,0:T(8,128)(2,1)} %get-tuple-element.12.refs_3_), channel_id=1, source_target_pairs={{0,2},{1,3},{2,0},{3,1},{4,6},{5,7},{6,4},{7,5},{8,10},{9,11},{10,... | collective-permute-start | bytes 110600 | tf_op jit(solution)/shard_map/ppermute | solution.py:383
  9.5 6.0 %collective-permute-start.1 = (bf16[2,72,128]{2,1,0:T(8,128)(2,1)}, bf16[2,72,128]{2,1,0:T(8,128)(2,1)S(1)}, u32[]{:S(2)}, u32[]{:S(2)}) collective-permute-start(bf16[2,72,128]{2,1,0:T(8,128)(2,1)} %get-tuple-element.12.refs_3_), channel_id=1, source_target_pairs={{0,1},{1,2},{2,3},{3,0},{4,5},{5,6},{6,7},{7,4},{8,9},{9,10},{10,1... | collective-permute-start | bytes 110600 | tf_op jit(solution)/shard_map/ppermute | solution.py:383
  15.5 0.9 %copy-start = (bf16[112,640]{1,0:T(8,128)(2,1)S(1)}, bf16[112,640]{1,0:T(8,128)(2,1)}, u32[]{:S(2)}) copy-start(bf16[112,640]{1,0:T(8,128)(2,1)} %get-tuple-element.10.refs_0_) | copy-start | bytes 430084
  16.4 0.8 %copy-start.2 = (bf16[32,640]{1,0:T(8,128)(2,1)S(1)}, bf16[32,640]{1,0:T(8,128)(2,1)}, u32[]{:S(2)}) copy-start(bf16[32,640]{1,0:T(8,128)(2,1)} %get-tuple-element.11.refs_2_) | copy-start | bytes 122884
  17.2 0.8 %copy-start.3 = (bf16[2,72,128]{2,1,0:T(8,128)(2,1)S(1)}, bf16[2,72,128]{2,1,0:T(8,128)(2,1)}, u32[]{:S(2)}) copy-start(bf16[2,72,128]{2,1,0:T(8,128)(2,1)} %get-tuple-element.12.refs_3_) | copy-start | bytes 110596
  33.1 0.7 %copy-start.1 = (f32[64,512]{1,0:T(8,128)}, f32[64,512]{1,0:T(8,128)S(1)}, u32[]{:S(2)}) copy-start(f32[64,512]{1,0:T(8,128)S(1)} %get-tuple-element.13.here_hbm) | copy-start | bytes 393220
  33.8 11.3 %collective-permute-start.4 = (f32[64,512]{1,0:T(8,128)S(1)}, f32[64,512]{1,0:T(8,128)S(1)}, u32[]{:S(2)}, u32[]{:S(2)}) collective-permute-start(f32[64,512]{1,0:T(8,128)S(1)} %get-tuple-element.14), channel_id=1, source_target_pairs={{0,4},{4,8},{8,12},{12,16},{16,20},{20,24},{24,28},{28,0},{1,5},{5... | collective-permute-start | bytes 393224 | tf_op jit(solution)/shard_map/ppermute | solution.py:421
  45.1 0.6 %copy-start.5 = (f32[64,512]{1,0:T(8,128)}, f32[64,512]{1,0:T(8,128)S(1)}, u32[]{:S(2)}) copy-start(f32[64,512]{1,0:T(8,128)S(1)} %collective-permute-done.4.came_hbm) | copy-start | bytes 393220

commit v4 on v3

--- a/solution.py
+++ b/solution.py
@@ -114,13 +114,10 @@
 
 
 def field_kernel(block, width, ksize, n_sets, weight_ref, *refs):
-    sources = refs[: 3 + n_sets]
-    here_ref, there_hbm, sums_ref = refs[3 + n_sets : 6 + n_sets]
-    landed = refs[6 + n_sets : 9 + 2 * n_sets]
-    own_ref, next_ref, rest_ref = landed[:3]
-    tap_refs = landed[3:]
+    own_ref, next_ref, rest_ref = refs[:3]
+    tap_refs = refs[3 : 3 + n_sets]
+    here_ref, there_ref, sums_ref = refs[3 + n_sets : 6 + n_sets]
     (
-        there_ref,
         taps32,
         mask_t,
         target_t,
@@ -133,9 +130,7 @@
         total_ref,
         spot_hits,
         slot_hits,
-        sems,
-        out_sem,
-    ) = refs[9 + 2 * n_sets :]
+    ) = refs[6 + n_sets :]
     radius = (ksize - 1) // 2
     per_set = tap_refs[0].shape[0]
     pairs = n_sets * per_set // 2
@@ -150,14 +145,6 @@
     kern_at = lax.axis_index("kern")
     last = lax.axis_index("tile") == lax.axis_size("tile") - 1
 
-    copies = [
-        pltpu.make_async_copy(source, place, sems.at[at])
-        for at, (source, place) in enumerate(zip(sources, landed))
-    ]
-    for copy in copies:
-        copy.start()
-    for copy in copies[3:]:
-        copy.wait()
     for index, ref in enumerate(tap_refs):
         taps32[index * per_set : (index + 1) * per_set] = ref[...].astype(F32)
 
@@ -182,8 +169,6 @@
         tail_band[component * rows : (component + 1) * rows, :] = toeplitz(component, ksize - 1)
     build(0, 0)
 
-    for copy in copies[:3]:
-        copy.wait()
     for piece in range(mask_t.shape[0] // LANES):
         lanes = slice(piece * LANES, (piece + 1) * LANES)
         both = jnp.concatenate([own_ref[0:rows, lanes], next_ref[0:rows, lanes]], 0)
@@ -286,8 +271,6 @@
         turned = tiles_of_total[piece].T
         here_ref[:, lanes] = turned[:rows]
         there_ref[:, lanes] = turned[rows:]
-    send = pltpu.make_async_copy(there_ref, there_hbm, out_sem)
-    send.start()
 
     two = jnp.concatenate(split2(jnp.concatenate(tiles_of_total, 1)), 0)
     picked = jnp.dot(two, spot_hits[...], preferred_element_type=F32)
@@ -303,18 +286,9 @@
         sums_ref[tile * n_sets : (tile + 1) * n_sets, :] = jnp.broadcast_to(
             sums[tile : tile + 1], (n_sets, slots)
         )
-    send.wait()
-
-
-def finish_kernel(here_hbm, came_hbm, got_hbm, grad_ref, sums_ref, here_ref, came_ref, got_ref, sems):
-    copies = [
-        pltpu.make_async_copy(source, place, sems.at[at])
-        for at, (source, place) in enumerate(((here_hbm, here_ref), (came_hbm, came_ref), (got_hbm, got_ref)))
-    ]
-    for copy in copies:
-        copy.start()
-    for copy in copies:
-        copy.wait()
+
+
+def finish_kernel(here_ref, came_ref, got_ref, grad_ref, sums_ref):
     grad_ref[...] = here_ref[...] + came_ref[...]
     sums_ref[...] = jnp.sum(got_ref[...], 0, keepdims=True)
 
@@ -366,16 +340,22 @@
             pltpu.VMEM((LANES, LANES), F32),
             pltpu.SemaphoreType.DMA((12,)),
         ],
+        compiler_params=pltpu.CompilerParams(vmem_limit_bytes=4 << 20),
         name="pack",
     )(
-        mask_field,
-        target_map,
-        kernel_real,
-        kernel_imag,
-        edge_pixel.reshape(tiled),
-        edge_owner.reshape(tiled),
-        edge_slot.reshape(tiled),
-        edge_weight.reshape(tiled),
+        *[
+            pltpu.with_memory_space_constraint(array, pltpu.HBM)
+            for array in (
+                mask_field,
+                target_map,
+                kernel_real,
+                kernel_imag,
+                edge_pixel.reshape(tiled),
+                edge_owner.reshape(tiled),
+                edge_slot.reshape(tiled),
+                edge_weight.reshape(tiled),
+            )
+        ]
     )
 
     following = lax.ppermute(own, "tile", [(i, (i - 1) % tiles) for i in range(tiles)])
@@ -393,11 +373,9 @@
             jax.ShapeDtypeStruct((rows, block), F32),
             jax.ShapeDtypeStruct((tiles * kerns, POLY_DEV), F32),
         ),
-        in_specs=[SMEM] + [HBM] * len(sources),
-        out_specs=(VMEM, HBM, VMEM),
-        scratch_shapes=[pltpu.VMEM(source.shape, source.dtype) for source in sources]
-        + [
-            pltpu.VMEM((rows, block), F32),
+        in_specs=[SMEM] + [VMEM] * len(sources),
+        out_specs=(VMEM,) * 3,
+        scratch_shapes=[
             pltpu.VMEM((components, tap_rows, LANES), F32),
             pltpu.VMEM((whole, LANES), F32),
             pltpu.VMEM((whole, LANES), F32),
@@ -410,8 +388,6 @@
             pltpu.VMEM((block, LANES), F32),
             pltpu.VMEM((block, 2 * edges), BF16),
             pltpu.VMEM((POLY_DEV, 2 * edges), BF16),
-            pltpu.SemaphoreType.DMA((len(sources),)),
-            pltpu.SemaphoreType.DMA,
         ],
         compiler_params=pltpu.CompilerParams(
             vmem_limit_bytes=groups * height * GROUP * LANES * 2 + (24 << 20)
@@ -426,14 +402,9 @@
             jax.ShapeDtypeStruct((rows, block), F32),
             jax.ShapeDtypeStruct((1, POLY_DEV), F32),
         ),
-        in_specs=[HBM] * 3,
+        in_specs=[VMEM] * 3,
         out_specs=(VMEM,) * 2,
-        scratch_shapes=[
-            pltpu.VMEM((rows, block), F32),
-            pltpu.VMEM((rows, block), F32),
-            pltpu.VMEM(got.shape, F32),
-            pltpu.SemaphoreType.DMA((3,)),
-        ],
+        compiler_params=pltpu.CompilerParams(vmem_limit_bytes=4 << 20),
         name="finish",
     )(here, came, got)
     return (mask_grad, sums.reshape(-1))

time: 47.7 us -> 39.2 us (0.82)
  local copies, waits for them, and re-layouts: 4.38 us -> 0.04 us
  Pallas kernels: 18.7 us -> 14.9 us
    unnamed x13 -> x3, local copies, waits for them, and re-layouts: 4.35 us -> 0.01 us
    pallas_call x1, Pallas kernels: 15.1 us -> 12.9 us  [on_device(): pl.pallas_call(functools.partial(field_kernel, block, width, ksize, kerns...]
    pallas_call x1, Pallas kernels: 1.66 us -> 0.67 us  [on_device(): pl.pallas_call(finish_kernel, out_shape=(jax.ShapeDtypeStruct((rows, bloc...]
    pallas_call x1, Pallas kernels: 1.88 us -> 1.27 us  [on_device(): pl.pallas_call(functools.partial(pack_kernel, block), out_shape=(jax.Shap...]
  transfers between devices with their start and end apart: 5 -> 5, of which waited for: 3 -> 3; matrix products, arithmetic and copies ran while one was open for 1% -> 0% of each run, Pallas kernels for 0% -> 0%
where the time goes in v4:
time: 39.2 us; the launch traced here: 39 us
  Pallas kernels  14.9 us (38%)
  blocking collectives  10.6 us (27%)
  starting transfers between devices  8.05 us (21%)
  waiting for transfers between devices  4.75 us (12%)
  between operations  0.66 us (2%)
    pallas_call x1, Pallas kernels, on_device(): pl.pallas_call(functools.partial(field_kernel, block, width, ksize, kerns...  12.9 us
    all_to_all x1, blocking collectives, on_device(): got = lax.all_to_all(sums, ('tile', 'kern'), 0, 0, tiled=True)  10.6 us
    ppermute x3, waiting for transfers between devices, on_device(): lax.ppermute(taps, 'kern', [(i, (i + step) % kerns) for i in range(kerns)])  4.74 us
    ppermute x3, starting transfers between devices, on_device(): lax.ppermute(taps, 'kern', [(i, (i + step) % kerns) for i in range(kerns)])  4.62 us
    ppermute x1, starting transfers between devices, on_device(): lax.ppermute(own, 'tile', [(i, (i - 1) % tiles) for i in range(tiles)])  3.39 us
    pallas_call x1, Pallas kernels, on_device(): pl.pallas_call(functools.partial(pack_kernel, block), out_shape=(jax.Shap...  1.27 us
  transfers between devices with their start and end apart: 5, of which 3 were waited for; matrix products, arithmetic and copies ran while one was open for 0% of the time, Pallas kernels for 0%

profile of v4, /device:TPU:0, one launch (start us, length us, event | category | flops | bytes accessed | tf_op | source)
XLA Modules:
  0.0 39.0 jit_solution(16680799284804655329)
XLA Ops:
  0.6 1.3 %pack.1 = (bf16[112,640]{1,0:T(8,128)(2,1)S(1)}, bf16[32,640]{1,0:T(8,128)(2,1)S(1)}, bf16[2,72,128]{2,1,0:T(8,128)(2,1)S(1)}) custom-call(bf16[64,2048]{1,0:T(8,128)(2,1)} %mask_hbm.1, s32[64,2048]{1,0:T(8,128)} %target_hbm.1, bf16[1,65,65]{2,1,0:T(8,128)(2,1)} %real_hbm.1, bf16[1,65,65]{2,1,0:T(8,128)(2,1)} %imag_hbm.1, s32[8,128]{1,0:T(8,128)} %bitcast.11, ...), custom_call_target="tpu_custom_call" | custom-call | tf_op jit(solution)/shard_map/pack/pallas_call | solution.py:322
  1.9 3.4 %collective-permute-start = (bf16[112,640]{1,0:T(8,128)(2,1)S(1)}, bf16[112,640]{1,0:T(8,128)(2,1)S(1)}, u32[]{:S(2)}, u32[]{:S(2)}) collective-permute-start(bf16[112,640]{1,0:T(8,128)(2,1)S(1)} %get-tuple-element.10.refs_0_), channel_id=1, source_target_pairs={{0,28},{4,0},{8,4},{12,8},{16,12},{20,16},{24,20},{28,24},{1,29},{... | collective-permute-start | bytes 430088 | tf_op jit(solution)/shard_map/ppermute | solution.py:361
  5.3 0.0 copy-start
  5.3 3.6 %collective-permute-start.3 = (bf16[2,72,128]{2,1,0:T(8,128)(2,1)S(1)}, bf16[2,72,128]{2,1,0:T(8,128)(2,1)S(1)}, u32[]{:S(2)}, u32[]{:S(2)}) collective-permute-start(bf16[2,72,128]{2,1,0:T(8,128)(2,1)S(1)} %get-tuple-element.12.refs_3_), channel_id=1, source_target_pairs={{0,3},{1,0},{2,1},{3,2},{4,7},{5,4},{6,5},{7,6},{8,11},{9,8},{10,9... | collective-permute-start | bytes 110600 | tf_op jit(solution)/shard_map/ppermute | solution.py:363
  8.9 0.0 collective-permute-start.2
  8.9 1.0 %collective-permute-start.1 = (bf16[2,72,128]{2,1,0:T(8,128)(2,1)S(1)}, bf16[2,72,128]{2,1,0:T(8,128)(2,1)S(1)}, u32[]{:S(2)}, u32[]{:S(2)}) collective-permute-start(bf16[2,72,128]{2,1,0:T(8,128)(2,1)S(1)} %get-tuple-element.12.refs_3_), channel_id=1, source_target_pairs={{0,1},{1,2},{2,3},{3,0},{4,5},{5,6},{6,7},{7,4},{8,9},{9,10},{10,1... | collective-permute-start | bytes 110600 | tf_op jit(solution)/shard_map/ppermute | solution.py:363
  9.9 0.6 %collective-permute-done.3.refs_6_ = bf16[2,72,128]{2,1,0:T(8,128)(2,1)S(1)} collective-permute-done((bf16[2,72,128]{2,1,0:T(8,128)(2,1)S(1)}, bf16[2,72,128]{2,1,0:T(8,128)(2,1)S(1)}, u32[]{:S(2)}, u32[]{:S(2)}) %collective-permute-start.3) | collective-permute-done | bytes 36896 | tf_op jit(solution)/shard_map/ppermute | solution.py:363
  10.5 3.2 %collective-permute-done.2.refs_5_ = bf16[2,72,128]{2,1,0:T(8,128)(2,1)S(1)} collective-permute-done((bf16[2,72,128]{2,1,0:T(8,128)(2,1)S(1)}, bf16[2,72,128]{2,1,0:T(8,128)(2,1)S(1)}, u32[]{:S(2)}, u32[]{:S(2)}) %collective-permute-start.2) | collective-permute-done | bytes 36896 | tf_op jit(solution)/shard_map/ppermute | solution.py:363
  13.8 0.9 %collective-permute-done.1.refs_4_ = bf16[2,72,128]{2,1,0:T(8,128)(2,1)S(1)} collective-permute-done((bf16[2,72,128]{2,1,0:T(8,128)(2,1)S(1)}, bf16[2,72,128]{2,1,0:T(8,128)(2,1)S(1)}, u32[]{:S(2)}, u32[]{:S(2)}) %collective-permute-start.1) | collective-permute-done | bytes 36896 | tf_op jit(solution)/shard_map/ppermute | solution.py:363
  14.7 0.0 collective-permute-done.refs_1_
  14.7 0.0 copy-done
  14.7 12.9 %fields.1 = (f32[64,512]{1,0:T(8,128)S(1)}, f32[64,512]{1,0:T(8,128)S(1)}, f32[32,256]{1,0:T(8,128)S(1)}) custom-call(f32[4]{0:T(128)S(1)} %copy-done, bf16[112,640]{1,0:T(8,128)(2,1)S(1)} %get-tuple-element.10.refs_0_, bf16[112,640]{1,0:T(8,128)(2,1)S(1)} %collective-permute-done.refs_1_, bf16[32,640]{1,0:T(8,128)(2,1)S(1)} %get-tuple-element.11.refs_2_, ...), custom_call_target="tpu_custom_call" | custom-call | tf_op jit(solution)/shard_map/fields/pallas_call | solution.py:369
  27.6 0.0 collective-permute-start.4
  27.7 10.6 %all_to_all.11 = f32[32,1,256]{2,1,0:T(1,128)S(1)} all-to-all(f32[32,1,256]{2,1,0:T(1,128)S(1)} %copy.11), channel_id=1, replica_groups=mesh['tile'=8,'kern'=4] {'tile','kern'}, dimensions={0} | all-to-all | bytes 65536 | tf_op jit(solution)/shard_map/all_to_all | solution.py:398
  38.3 0.0 collective-permute-done.4.came_ref
  38.3 0.7 %finish.1 = (f32[64,512]{1,0:T(8,128)}, f32[1,256]{1,0:T(1,128)}) custom-call(f32[64,512]{1,0:T(8,128)S(1)} %get-tuple-element.13.here_ref, f32[64,512]{1,0:T(8,128)S(1)} %collective-permute-done.4.came_ref, f32[32,256]{1,0:T(8,128)S(1)} %bitcast.9), custom_call_target="tpu_custom_call" | custom-call | tf_op jit(solution)/shard_map/finish/pallas_call | solution.py:399
  (2 shorter events, 0.0 us)
Async XLA Ops:
  1.9 12.8 %collective-permute-start = (bf16[112,640]{1,0:T(8,128)(2,1)S(1)}, bf16[112,640]{1,0:T(8,128)(2,1)S(1)}, u32[]{:S(2)}, u32[]{:S(2)}) collective-permute-start(bf16[112,640]{1,0:T(8,128)(2,1)S(1)} %get-tuple-element.10.refs_0_), channel_id=1, source_target_pairs={{0,28},{4,0},{8,4},{12,8},{16,12},{20,16},{24,20},{28,24},{1,29},{... | collective-permute-start | bytes 430088 | tf_op jit(solution)/shard_map/ppermute | solution.py:361
  5.3 9.4 %copy-start = (f32[4]{0:T(128)S(1)}, f32[4]{0:T(128)}, u32[]{:S(2)}) copy-start(f32[4]{0:T(128)} %weight_ref.1) | copy-start | bytes 52
  5.3 5.2 %collective-permute-start.3 = (bf16[2,72,128]{2,1,0:T(8,128)(2,1)S(1)}, bf16[2,72,128]{2,1,0:T(8,128)(2,1)S(1)}, u32[]{:S(2)}, u32[]{:S(2)}) collective-permute-start(bf16[2,72,128]{2,1,0:T(8,128)(2,1)S(1)} %get-tuple-element.12.refs_3_), channel_id=1, source_target_pairs={{0,3},{1,0},{2,1},{3,2},{4,7},{5,4},{6,5},{7,6},{8,11},{9,8},{10,9... | collective-permute-start | bytes 110600 | tf_op jit(solution)/shard_map/ppermute | solution.py:363
  8.9 4.9 %collective-permute-start.2 = (bf16[2,72,128]{2,1,0:T(8,128)(2,1)S(1)}, bf16[2,72,128]{2,1,0:T(8,128)(2,1)S(1)}, u32[]{:S(2)}, u32[]{:S(2)}) collective-permute-start(bf16[2,72,128]{2,1,0:T(8,128)(2,1)S(1)} %get-tuple-element.12.refs_3_), channel_id=1, source_target_pairs={{0,2},{1,3},{2,0},{3,1},{4,6},{5,7},{6,4},{7,5},{8,10},{9,11},{10,... | collective-permute-start | bytes 110600 | tf_op jit(solution)/shard_map/ppermute | solution.py:363
  8.9 5.8 %collective-permute-start.1 = (bf16[2,72,128]{2,1,0:T(8,128)(2,1)S(1)}, bf16[2,72,128]{2,1,0:T(8,128)(2,1)S(1)}, u32[]{:S(2)}, u32[]{:S(2)}) collective-permute-start(bf16[2,72,128]{2,1,0:T(8,128)(2,1)S(1)} %get-tuple-element.12.refs_3_), channel_id=1, source_target_pairs={{0,1},{1,2},{2,3},{3,0},{4,5},{5,6},{6,7},{7,4},{8,9},{9,10},{10,1... | collective-permute-start | bytes 110600 | tf_op jit(solution)/shard_map/ppermute | solution.py:363
  27.6 10.8 %collective-permute-start.4 = (f32[64,512]{1,0:T(8,128)S(1)}, f32[64,512]{1,0:T(8,128)S(1)}, u32[]{:S(2)}, u32[]{:S(2)}) collective-permute-start(f32[64,512]{1,0:T(8,128)S(1)} %get-tuple-element.14), channel_id=1, source_target_pairs={{0,4},{4,8},{8,12},{12,16},{16,20},{20,24},{24,28},{28,0},{1,5},{5... | collective-permute-start | bytes 393224 | tf_op jit(solution)/shard_map/ppermute | solution.py:397

commit v5 on v4

v5 whole, which is shorter than its diff:
```python
import functools

import jax
import jax.numpy as jnp
from jax import lax
from jax.experimental import pallas as pl
from jax.experimental.pallas import tpu as pltpu
from jax.sharding import PartitionSpec as P

POLY_DEV = 256

steepness = 8.0
threshold = 0.67

F32 = jnp.float32
BF16 = jnp.bfloat16
LANES = 128
SIDE = 64
GROUP = 16
FACTS = 7
HBM = pl.BlockSpec(memory_space=pltpu.HBM)
VMEM = pl.BlockSpec(memory_space=pltpu.VMEM)


def split3(value):
    high = value.astype(BF16)
    rest = value - high.astype(F32)
    middle = rest.astype(BF16)
    low = (rest - middle.astype(F32)).astype(BF16)
    return high, middle, low


def split2(value):
    high = value.astype(BF16)
    return high, (value - high.astype(F32)).astype(BF16)


def pack_kernel(
    block,
    mask_hbm,
    target_hbm,
    real_hbm,
    imag_hbm,
    pixel_hbm,
    owner_hbm,
    slot_hbm,
    weight_hbm,
    socs_hbm,
    out_ref,
    rest_ref,
    taps_ref,
    socs_ref,
    mask_ref,
    target_ref,
    real_ref,
    imag_ref,
    pixel_ref,
    owner_ref,
    slot_ref,
    weight_ref,
    socs_smem,
    square,
    sems,
):
    rows, width = mask_hbm.shape
    half = rows // 2
    first = lax.axis_index("kern") * block
    left = pl.multiple_of(jnp.maximum(first - LANES, 0), LANES)
    right = pl.multiple_of(jnp.minimum(first + block, width - LANES), LANES)
    middle = pl.multiple_of(first, LANES)
    copies = []

    def fetch(source, place):
        copies.append(pltpu.make_async_copy(source, place, sems.at[len(copies)]))
        copies[-1].start()

    for source, place in ((mask_hbm, mask_ref), (target_hbm, target_ref)):
        fetch(source.at[:, pl.ds(middle, block)], place.at[:, LANES : LANES + block])
        fetch(source.at[:, pl.ds(left, LANES)], place.at[:, 0:LANES])
        fetch(source.at[:, pl.ds(right, LANES)], place.at[:, LANES + block :])
    fetch(real_hbm, real_ref)
    fetch(imag_hbm, imag_ref)
    fetch(pixel_hbm, pixel_ref)
    fetch(owner_hbm, owner_ref)
    fetch(slot_hbm, slot_ref)
    fetch(weight_hbm, weight_ref)
    fetch(socs_hbm, socs_smem)
    square[...] = jnp.zeros_like(square)
    for copy in copies:
        copy.wait()

    whole = block + 2 * SIDE
    cut = slice(LANES - SIDE, LANES - SIDE + whole)
    column = first - SIDE + lax.broadcasted_iota(jnp.int32, (rows, whole), 1)
    inside = jnp.logical_and(column >= 0, column < width)
    mask = jnp.where(inside, mask_ref[...].astype(F32)[:, cut], 0.0)
    out_ref[0:rows, :] = mask.astype(BF16)
    target = target_ref[...].astype(F32)[:, cut].astype(BF16)
    out_ref[rows : rows + half, :] = target[:half]
    rest_ref[...] = target[half:]

    pixel = pixel_ref[...]
    pixel_high = pixel // LANES
    facts = [pixel_high, pixel - pixel_high * LANES, owner_ref[...], slot_ref[...]]
    facts = [fact.astype(F32) for fact in facts] + [part.astype(F32) for part in split3(weight_ref[...])]
    beside = whole // LANES
    layers = (out_ref.shape[0] - rows - half) // facts[0].shape[0]
    facts += [jnp.zeros_like(facts[0])] * (layers * beside - len(facts))
    lines = [jnp.concatenate(facts[at * beside : (at + 1) * beside], 1) for at in range(layers)]
    out_ref[rows + half :, :] = jnp.concatenate(lines, 0).astype(BF16)

    count = real_ref.shape[0]
    kernels = socs_hbm.shape[0]
    total_weight = socs_smem[0]
    for kernel in range(1, kernels):
        total_weight = total_weight + socs_smem[kernel]
    for index in range(kernels // count):
        source = lax.bitwise_xor(lax.axis_index("kern"), jnp.int32(index)) * count
        for kernel in range(count):
            at = index * count + kernel
            socs_ref[at : at + 1, :] = jnp.full((1, LANES), socs_smem[source + kernel], F32)
    socs_ref[kernels : kernels + 1, :] = jnp.full((1, LANES), total_weight, F32)

    ksize = real_ref.shape[1]
    for kernel in range(real_ref.shape[0]):
        for part, ref in enumerate((real_ref, imag_ref)):
            square[0:ksize, 0:ksize] = ref[kernel].astype(F32)
            taps_ref[2 * kernel + part] = square[...].T[: taps_ref.shape[1]].astype(BF16)


def band_maker(ksize, tap_refs, taps32):
    per_set = tap_refs[0].shape[0]
    rows = LANES // 2
    window = 2 * rows
    last = lax.axis_index("tile") == lax.axis_size("tile") - 1
    for index, ref in enumerate(tap_refs):
        taps32[index * per_set : (index + 1) * per_set] = ref[...].astype(F32)

    out_row = lax.broadcasted_iota(jnp.int32, (rows, window), 0) < rows // 2
    in_row = lax.broadcasted_iota(jnp.int32, (rows, window), 1) < rows
    keep = jnp.logical_or(out_row == in_row, jnp.logical_not(last))
    keep = keep.astype(F32)

    def toeplitz(component, b):
        row = jnp.broadcast_to(taps32[component, b : b + 1, :], (rows, window))
        return (pltpu.roll(row, 0, 1, stride=1, stride_axis=0) * keep).astype(BF16)

    return toeplitz


def shift_mask(mask_t, shifted):
    tall = mask_t.shape[0]
    for j in range(GROUP):
        count = tall if j == 0 else tall - GROUP
        shifted[0:count, j * LANES : (j + 1) * LANES] = mask_t[j : j + count, :].astype(BF16)


def half_fields(ksize, toeplitz, base, offset, shifted, band, tail_band, fields):
    height = tail_band.shape[0]
    rows = LANES // 2
    components = height // rows
    window = 2 * rows
    radius = (ksize - 1) // 2
    span = fields.shape[0]
    groups = (ksize - 1) // GROUP
    part = GROUP // 2

    def build(group, side):
        for j in range(side * part, (side + 1) * part):
            for component in range(components):
                top = offset + group * height + component * rows
                band[top : top + rows, j * window : (j + 1) * window] = toeplitz(
                    base + component, group * GROUP + j
                )

    for component in range(components):
        tail_band[component * rows : (component + 1) * rows, :] = toeplitz(base + component, ksize - 1)
    build(0, 0)
    nt = (((1,), (1,)), ((), ()))
    fields[...] = lax.dot_general(
        shifted[2 * radius :, 0:window], tail_band[...], nt, preferred_element_type=F32
    )
    steps = [(group, side) for group in range(groups) for side in range(2)]
    for at, (group, side) in enumerate(steps):
        if at + 1 < len(steps):
            build(*steps[at + 1])
        lanes = slice(side * part * window, (side + 1) * part * window)
        top = offset + group * height
        fields[...] += lax.dot_general(
            shifted[group * GROUP : group * GROUP + span, lanes],
            band[top : top + height, lanes],
            nt,
            preferred_element_type=F32,
        )


def first_kernel(ksize, own_ref, next_ref, *refs):
    mask_t, fields, shifted, band, tail_band, taps32 = refs[-6:]
    tap_refs = refs[:-6]
    rows = LANES // 2
    for piece in range(mask_t.shape[0] // LANES):
        lanes = slice(piece * LANES, (piece + 1) * LANES)
        both = jnp.concatenate([own_ref[0:rows, lanes], next_ref[0:rows, lanes]], 0)
        mask_t[lanes, :] = both.astype(F32).T
    shift_mask(mask_t, shifted)
    toeplitz = band_maker(ksize, tap_refs, taps32)
    half_fields(ksize, toeplitz, 0, 0, shifted, band, tail_band, fields)


def second_kernel(block, width, ksize, n_sets, weight_ref, own_ref, next_ref, rest_ref, *refs):
    mask_t, fields_a = refs[:2]
    tap_refs = refs[2 : 2 + n_sets]
    here_ref, there_ref, sums_ref = refs[2 + n_sets : 5 + n_sets]
    (
        taps32,
        target_t,
        shifted,
        band,
        tail_a,
        tail_b,
        fields_b,
        products,
        parts,
        total_ref,
        spot_hits,
        slot_hits,
    ) = refs[5 + n_sets :]
    radius = (ksize - 1) // 2
    per_set = tap_refs[0].shape[0]
    pairs = n_sets * per_set // 2
    rows = here_ref.shape[0]
    half = rows // 2
    window = 2 * rows
    span = block + 2 * radius
    tall_out = block + GROUP
    groups = (ksize - 1) // GROUP
    height = tail_a.shape[0]
    deep_k = groups * height
    kern_at = lax.axis_index("kern")
    nt = (((1,), (1,)), ((), ()))

    shift_mask(mask_t, shifted)
    for piece in range(target_t.shape[0] // LANES):
        lanes = slice(piece * LANES, (piece + 1) * LANES)
        one = jnp.concatenate([rest_ref[:, lanes], next_ref[rows : rows + half, lanes]], 0)
        target_t[lanes, :] = jnp.concatenate([one, one], 0).astype(F32).T
    toeplitz = band_maker(ksize, tap_refs, taps32)
    half_fields(ksize, toeplitz, pairs, deep_k, shifted, band, tail_b, fields_b)

    def field(kernel):
        from_ref = (fields_a, fields_b)[kernel // (pairs // 2)]
        left = kernel % (pairs // 2) * window
        return from_ref[:, left : left + window]

    @pl.when(kern_at >= 0)
    def _():
        def rebuild(j):
            for group in range(groups):
                for component in range(pairs):
                    top = group * height + component * rows
                    band[top : top + rows, j * window : (j + 1) * window] = toeplitz(
                        component, group * GROUP + j
                    )

        for component in range(pairs):
            tail_a[component * rows : (component + 1) * rows, :] = toeplitz(component, ksize - 1)
        rebuild(0)
        rebuild(1)

        weights = [weight_ref[kernel : kernel + 1, :] for kernel in range(pairs)]
        total_weight = weight_ref[pairs : pairs + 1, :]
        intensity = jnp.zeros((span, window), F32)
        for kernel in range(pairs):
            intensity = intensity + weights[kernel] * field(kernel) * field(kernel)
        intensity = intensity + pltpu.roll(intensity, rows, 1)
        resist = jax.nn.sigmoid(steepness * (intensity / total_weight - threshold))
        target = target_t[SIDE - radius : SIDE - radius + span, :]
        slope = 2.0 * (resist - target) * steepness * resist * (1.0 - resist) / total_weight
        column = kern_at * block - radius + lax.broadcasted_iota(jnp.int32, (span, window), 0)
        slope = jnp.where(jnp.logical_and(column >= 0, column < width), slope, 0.0)
        for kernel in range(pairs):
            value = ((2.0 * weights[kernel]) * slope * field(kernel)).astype(BF16)
            for group in range(groups):
                skip = (groups - 1 - group) * GROUP
                left = (kernel // (pairs // 2) * groups + group) * height + kernel % (pairs // 2) * window
                products[:, left : left + window] = value[skip : skip + tall_out]

        beside = own_ref.shape[1] // LANES
        deep = 8

        def fact(index):
            top, left = index // beside * deep, index % beside * LANES
            lines = []
            for ref in (own_ref, next_ref):
                tile = ref[rows + half :, :].astype(F32)[top : top + deep, left : left + LANES]
                lines += [tile[at : at + 1] for at in range(deep)]
            return jnp.concatenate(lines, 1)

        pixel = (fact(0) * LANES + fact(1)).astype(jnp.int32)
        owner = fact(2).astype(jnp.int32)
        slot = fact(3).astype(jnp.int32)
        edge_weight = fact(4) + fact(5) + fact(6)
        edges = pixel.shape[1]
        row = pixel // block
        col = pixel - row * block
        piece = col // LANES
        col = col - piece * LANES
        row = row + jnp.where(lax.broadcasted_iota(jnp.int32, (1, edges), 1) < edges // 2, 0, rows)
        pieces = block // LANES
        spot = piece * window + row
        spot_hits[...] = (
            (lax.broadcasted_iota(jnp.int32, (pieces * window, edges), 0) == spot).astype(F32).astype(BF16)
        )
        slots = slot_hits.shape[0]
        slot_hits[...] = (lax.broadcasted_iota(jnp.int32, (slots, edges), 0) == slot).astype(F32).astype(BF16)

        def moved(j):
            return parts[j, GROUP - j : GROUP - j + block, :]

        total_ref[...] = jnp.dot(
            products[0:block, deep_k - height : deep_k], tail_a[...], preferred_element_type=F32
        ) + jnp.dot(products[0:block, 2 * deep_k - height :], tail_b[...], preferred_element_type=F32)
        for j in range(0, GROUP, 2):
            if j + 2 < GROUP:
                rebuild(j + 2)
                rebuild(j + 3)
            two = jnp.dot(products[...], band[:, j * window : (j + 2) * window], preferred_element_type=F32)
            parts[j] = two[:, :window]
            parts[j + 1] = two[:, window:]
            if j >= 2:
                total_ref[...] += moved(j - 2) + moved(j - 1)
        total = total_ref[...] + moved(GROUP - 2) + moved(GROUP - 1)
        tiles_of_total = [total[piece * LANES : (piece + 1) * LANES, :] for piece in range(pieces)]
        for piece in range(pieces):
            lanes = slice(piece * LANES, (piece + 1) * LANES)
            turned = tiles_of_total[piece].T
            here_ref[:, lanes] = turned[:rows]
            there_ref[:, lanes] = turned[rows:]

        two = jnp.concatenate(split2(jnp.concatenate(tiles_of_total, 1)), 0)
        picked = jnp.dot(two, spot_hits[...], preferred_element_type=F32)
        picked = picked[:LANES] + picked[LANES:]
        col_hit = lax.broadcasted_iota(jnp.int32, (LANES, edges), 0) == col
        value = jnp.sum(jnp.where(col_hit, picked, 0.0), 0, keepdims=True) * edge_weight
        tiles = sums_ref.shape[0] // n_sets
        spread = jnp.where(lax.broadcasted_iota(jnp.int32, (tiles, edges), 0) == owner, value, 0.0)
        spread = jnp.concatenate([part.astype(F32) for part in split2(spread)], 0).astype(BF16)
        sums = lax.dot_general(spread, slot_hits[...], nt, preferred_element_type=F32)
        sums = sums[:tiles] + sums[tiles:]
        for tile in range(tiles):
            sums_ref[tile * n_sets : (tile + 1) * n_sets, :] = jnp.broadcast_to(
                sums[tile : tile + 1], (n_sets, slots)
            )


def finish_kernel(here_ref, came_ref, got_ref, grad_ref, sums_ref):
    grad_ref[...] = here_ref[...] + came_ref[...]
    sums_ref[...] = jnp.sum(got_ref[...], 0, keepdims=True)


def on_device(
    mask_field,
    target_map,
    kernel_real,
    kernel_imag,
    socs_weight,
    edge_pixel,
    edge_owner,
    edge_slot,
    edge_weight,
):
    rows, width = mask_field.shape
    half = rows // 2
    count, ksize = kernel_real.shape[:2]
    tiles, kerns = lax.axis_size("tile"), lax.axis_size("kern")
    block = width // kerns
    radius = (ksize - 1) // 2
    span = block + 2 * radius
    whole = block + 2 * SIDE
    groups = (ksize - 1) // GROUP
    edges = edge_pixel.shape[0]
    tap_rows = -(-ksize // 8) * 8
    layers = -(-FACTS // (whole // LANES))
    layers += layers % 2
    message = rows + half + layers * 8
    tiled = (edges // LANES, LANES)
    own, rest, taps, weights = pl.pallas_call(
        functools.partial(pack_kernel, block),
        out_shape=(
            jax.ShapeDtypeStruct((message, whole), BF16),
            jax.ShapeDtypeStruct((half, whole), BF16),
            jax.ShapeDtypeStruct((2 * count, tap_rows, LANES), BF16),
            jax.ShapeDtypeStruct((-(-(count * kerns + 1) // 8) * 8, LANES), F32),
        ),
        in_specs=[HBM] * 9,
        out_specs=(VMEM,) * 4,
        scratch_shapes=[
            pltpu.VMEM((rows, block + 2 * LANES), BF16),
            pltpu.VMEM((rows, block + 2 * LANES), jnp.int32),
            pltpu.VMEM(kernel_real.shape, BF16),
            pltpu.VMEM(kernel_imag.shape, BF16),
            pltpu.VMEM(tiled, jnp.int32),
            pltpu.VMEM(tiled, jnp.int32),
            pltpu.VMEM(tiled, jnp.int32),
            pltpu.VMEM(tiled, F32),
            pltpu.SMEM(socs_weight.shape, F32),
            pltpu.VMEM((LANES, LANES), F32),
            pltpu.SemaphoreType.DMA((13,)),
        ],
        compiler_params=pltpu.CompilerParams(vmem_limit_bytes=4 << 20),
        name="pack",
    )(
        *[
            pltpu.with_memory_space_constraint(array, pltpu.HBM)
            for array in (
                mask_field,
                target_map,
                kernel_real,
                kernel_imag,
                edge_pixel.reshape(tiled),
                edge_owner.reshape(tiled),
                edge_slot.reshape(tiled),
                edge_weight.reshape(tiled),
                socs_weight,
            )
        ]
    )

    following = lax.ppermute(own, "tile", [(i, (i - 1) % tiles) for i in range(tiles)])
    tap_sets = [taps] + [
        lax.ppermute(taps, "kern", [(i, i ^ step) for i in range(kerns)])
        for step in range(1, kerns)
    ]
    components = 2 * count * kerns // 2
    height = components * rows
    tall = span + 2 * radius
    band_shape = (groups * height, GROUP * LANES)
    band_bytes = groups * height * GROUP * LANES * 2
    macs = span * ksize * LANES * height
    mask_t, fields = pl.pallas_call(
        functools.partial(first_kernel, ksize),
        out_shape=(
            jax.ShapeDtypeStruct((whole, LANES), F32),
            jax.ShapeDtypeStruct((span, height), F32),
        ),
        in_specs=[VMEM] * (2 + kerns // 2),
        out_specs=(VMEM,) * 2,
        scratch_shapes=[
            pltpu.VMEM((tall, GROUP * LANES), BF16),
            pltpu.VMEM(band_shape, BF16),
            pltpu.VMEM((height, LANES), BF16),
            pltpu.VMEM((components, tap_rows, LANES), F32),
        ],
        compiler_params=pltpu.CompilerParams(vmem_limit_bytes=band_bytes + (12 << 20)),
        cost_estimate=pl.CostEstimate(flops=2 * macs, bytes_accessed=4 * span * height, transcendentals=0),
        name="first",
    )(own, following, *tap_sets[: kerns // 2])
    here, there, sums = pl.pallas_call(
        functools.partial(second_kernel, block, width, ksize, kerns),
        out_shape=(
            jax.ShapeDtypeStruct((rows, block), F32),
            jax.ShapeDtypeStruct((rows, block), F32),
            jax.ShapeDtypeStruct((tiles * kerns, POLY_DEV), F32),
        ),
        in_specs=[VMEM] * (6 + kerns),
        out_specs=(VMEM,) * 3,
        scratch_shapes=[
            pltpu.VMEM((2 * components, tap_rows, LANES), F32),
            pltpu.VMEM((whole, LANES), F32),
            pltpu.VMEM((tall, GROUP * LANES), BF16),
            pltpu.VMEM((2 * band_shape[0], band_shape[1]), BF16),
            pltpu.VMEM((height, LANES), BF16),
            pltpu.VMEM((height, LANES), BF16),
            pltpu.VMEM((span, height), F32),
            pltpu.VMEM((block + GROUP, 2 * groups * height), BF16),
            pltpu.VMEM((GROUP, block + GROUP, LANES), F32),
            pltpu.VMEM((block, LANES), F32),
            pltpu.VMEM((block, 2 * edges), BF16),
            pltpu.VMEM((POLY_DEV, 2 * edges), BF16),
        ],
        compiler_params=pltpu.CompilerParams(vmem_limit_bytes=2 * band_bytes + (24 << 20)),
        cost_estimate=pl.CostEstimate(flops=6 * macs, bytes_accessed=4 * span * height, transcendentals=0),
        name="fields",
    )(weights, own, following, rest, mask_t, fields, *tap_sets)
    came = lax.ppermute(there, "tile", [(i, (i + 1) % tiles) for i in range(tiles)])
    got = lax.all_to_all(sums, ("tile", "kern"), 0, 0, tiled=True)
    mask_grad, sums = pl.pallas_call(
        finish_kernel,
        out_shape=(
            jax.ShapeDtypeStruct((rows, block), F32),
            jax.ShapeDtypeStruct((1, POLY_DEV), F32),
        ),
        in_specs=[VMEM] * 3,
        out_specs=(VMEM,) * 2,
        compiler_params=pltpu.CompilerParams(vmem_limit_bytes=4 << 20),
        name="finish",
    )(here, came, got)
    return (mask_grad, sums.reshape(-1))


def solution(mesh):
    placed = (
        P("tile", None),
        P("tile", None),
        P("kern", None, None),
        P("kern", None, None),
        P(),
        P(("tile", "kern")),
        P(("tile", "kern"), None),
        P(("tile", "kern")),
        P(("tile", "kern")),
    )
    return jax.shard_map(
        on_device,
        mesh=mesh,
        in_specs=placed,
        out_specs=(P("tile", "kern"), P("tile")),
        check_vma=False,
    )
```

time: 39.2 us -> 37.6 us (0.959)
  waiting for transfers between devices: 4.75 us -> 1.55 us
  blocking collectives: 10.6 us -> 11.8 us
  Pallas kernels: 14.9 us -> 15.8 us
  starting transfers between devices: 8.05 us -> 7.57 us
    ppermute x3, waiting for transfers between devices: 4.74 us -> 1.55 us  [on_device(): lax.ppermute(taps, 'kern', [(i, i ^ step) for i in range(kerns)])]
    all_to_all x1, blocking collectives: 10.6 us -> 11.8 us  [on_device(): got = lax.all_to_all(sums, ('tile', 'kern'), 0, 0, tiled=True)]
    pallas_call x1 -> x2, Pallas kernels: 12.9 us -> 13.9 us  [the longest x1 10.3 us: on_device(): pl.pallas_call(functools.partial(second_kernel, block, width, ksize, kern...]
    ppermute x3, starting transfers between devices: 4.62 us -> 4.17 us  [on_device(): lax.ppermute(taps, 'kern', [(i, i ^ step) for i in range(kerns)])]
  transfers between devices with their start and end apart: 5 -> 5, of which waited for: 3 -> 1; matrix products, arithmetic and copies ran while one was open for 0% -> 0% of each run, Pallas kernels for 0% -> 10%
where the time goes in v5:
time: 37.6 us; the launch traced here: 37.5 us
  Pallas kernels  15.8 us (42%)
  blocking collectives  11.8 us (31%)
  starting transfers between devices  7.57 us (20%)
  waiting for transfers between devices  1.55 us (4%)
  between operations  0.68 us (2%)
    all_to_all x1, blocking collectives, on_device(): got = lax.all_to_all(sums, ('tile', 'kern'), 0, 0, tiled=True)  11.8 us
    pallas_call x1, Pallas kernels, on_device(): pl.pallas_call(functools.partial(second_kernel, block, width, ksize, kern...  10.3 us
    ppermute x3, starting transfers between devices, on_device(): lax.ppermute(taps, 'kern', [(i, i ^ step) for i in range(kerns)])  4.17 us
    pallas_call x1, Pallas kernels, on_device(): pl.pallas_call(functools.partial(first_kernel, ksize), out_shape=(jax.Sha...  3.57 us
    ppermute x1, starting transfers between devices, on_device(): lax.ppermute(own, 'tile', [(i, (i - 1) % tiles) for i in range(tiles)])  3.39 us
    ppermute x3, waiting for transfers between devices, on_device(): lax.ppermute(taps, 'kern', [(i, i ^ step) for i in range(kerns)])  1.55 us
    pallas_call x1, Pallas kernels, on_device(): pl.pallas_call(functools.partial(pack_kernel, block), out_shape=(jax.Shap...  1.28 us
  transfers between devices with their start and end apart: 5, of which 1 were waited for; matrix products, arithmetic and copies ran while one was open for 0% of the time, Pallas kernels for 10%

profile of v5, /device:TPU:0, one launch (start us, length us, event | category | flops | bytes accessed | tf_op | source)
XLA Modules:
  0.0 37.5 jit_solution(18105283675444955324)
XLA Ops:
  0.6 1.3 %pack.1 = (bf16[112,640]{1,0:T(8,128)(2,1)S(1)}, bf16[32,640]{1,0:T(8,128)(2,1)S(1)}, bf16[2,72,128]{2,1,0:T(8,128)(2,1)S(1)}, f32[8,128]{1,0:T(8,128)S(1)}) custom-call(bf16[64,2048]{1,0:T(8,128)(2,1)} %mask_hbm.1, s32[64,2048]{1,0:T(8,128)} %target_hbm.1, bf16[1,65,65]{2,1,0:T(8,128)(2,1)} %real_hbm.1, bf16[1,65,65]{2,1,0:T(8,128)(2,1)} %imag_hbm.1, ...), custom_call_target="tpu_custom_call" | custom-call | tf_op jit(solution)/shard_map/pack/pallas_call | solution.py:387
  1.9 3.4 %collective-permute-start = (bf16[112,640]{1,0:T(8,128)(2,1)S(1)}, bf16[112,640]{1,0:T(8,128)(2,1)S(1)}, u32[]{:S(2)}, u32[]{:S(2)}) collective-permute-start(bf16[112,640]{1,0:T(8,128)(2,1)S(1)} %get-tuple-element.14.own_ref), channel_id=1, source_target_pairs={{0,28},{4,0},{8,4},{12,8},{16,12},{20,16},{24,20},{28,24},{1,29},{... | collective-permute-start | bytes 430088 | tf_op jit(solution)/shard_map/ppermute | solution.py:429
  5.3 1.6 %collective-permute-start.1 = (bf16[2,72,128]{2,1,0:T(8,128)(2,1)S(1)}, bf16[2,72,128]{2,1,0:T(8,128)(2,1)S(1)}, u32[]{:S(2)}, u32[]{:S(2)}) collective-permute-start(bf16[2,72,128]{2,1,0:T(8,128)(2,1)S(1)} %get-tuple-element.16.refs_0_.refs_2_), channel_id=1, source_target_pairs={{0,1},{1,0},{2,3},{3,2},{4,5},{5,4},{6,7},{7,6},{8,9},{9,8},{10,11... | collective-permute-start | bytes 110600 | tf_op jit(solution)/shard_map/ppermute | solution.py:431
  6.9 2.5 %collective-permute-start.3 = (bf16[2,72,128]{2,1,0:T(8,128)(2,1)S(1)}, bf16[2,72,128]{2,1,0:T(8,128)(2,1)S(1)}, u32[]{:S(2)}, u32[]{:S(2)}) collective-permute-start(bf16[2,72,128]{2,1,0:T(8,128)(2,1)S(1)} %get-tuple-element.16.refs_0_.refs_2_), channel_id=1, source_target_pairs={{0,3},{1,2},{2,1},{3,0},{4,7},{5,6},{6,5},{7,4},{8,11},{9,10},{10,... | collective-permute-start | bytes 110600 | tf_op jit(solution)/shard_map/ppermute | solution.py:431
  9.4 0.1 collective-permute-start.2
  9.5 0.0 collective-permute-done.1.refs_1_.refs_3_
  9.5 0.0 collective-permute-done.next_ref
  9.5 3.6 %first.1 = (f32[640,128]{1,0:T(8,128)S(1)}, f32[576,256]{1,0:T(8,128)S(1)}) custom-call(bf16[112,640]{1,0:T(8,128)(2,1)S(1)} %get-tuple-element.14.own_ref, bf16[112,640]{1,0:T(8,128)(2,1)S(1)} %collective-permute-done.next_ref, bf16[2,72,128]{2,1,0:T(8,128)(2,1)S(1)} %get-tuple-element.16.refs_0_.refs_2_, ...), custom_call_target="tpu_custom_call" | custom-call | flops 2453667840 | bytes 589824 | tf_op jit(solution)/shard_map/first/pallas_call | solution.py:440
  13.1 0.0 collective-permute-done.3.refs_5_
  13.1 1.5 %collective-permute-done.2.refs_4_ = bf16[2,72,128]{2,1,0:T(8,128)(2,1)S(1)} collective-permute-done((bf16[2,72,128]{2,1,0:T(8,128)(2,1)S(1)}, bf16[2,72,128]{2,1,0:T(8,128)(2,1)S(1)}, u32[]{:S(2)}, u32[]{:S(2)}) %collective-permute-start.2) | collective-permute-done | bytes 36896 | tf_op jit(solution)/shard_map/ppermute | solution.py:431
  14.6 10.3 %fields.1 = (f32[64,512]{1,0:T(8,128)S(1)}, f32[64,512]{1,0:T(8,128)S(1)}, f32[32,256]{1,0:T(8,128)S(1)}) custom-call(f32[8,128]{1,0:T(8,128)S(1)} %get-tuple-element.13.weight_ref, bf16[112,640]{1,0:T(8,128)(2,1)S(1)} %get-tuple-element.14.own_ref, bf16[112,640]{1,0:T(8,128)(2,1)S(1)} %collective-permute-done.next_ref, ...), custom_call_target="tpu_custom_call" | custom-call | flops 7361003520 | bytes 589824 | tf_op jit(solution)/shard_map/fields/pallas_call | solution.py:458
  24.9 0.0 collective-permute-start.4
  25.0 11.8 %all_to_all.11 = f32[32,1,256]{2,1,0:T(1,128)S(1)} all-to-all(f32[32,1,256]{2,1,0:T(1,128)S(1)} %copy.11), channel_id=1, replica_groups=mesh['tile'=8,'kern'=4] {'tile','kern'}, dimensions={0} | all-to-all | bytes 65536 | tf_op jit(solution)/shard_map/all_to_all | solution.py:486
  36.8 0.0 collective-permute-done.4.came_ref
  36.8 0.7 %finish.1 = (f32[64,512]{1,0:T(8,128)}, f32[1,256]{1,0:T(1,128)}) custom-call(f32[64,512]{1,0:T(8,128)S(1)} %get-tuple-element.19.here_ref, f32[64,512]{1,0:T(8,128)S(1)} %collective-permute-done.4.came_ref, f32[32,256]{1,0:T(8,128)S(1)} %bitcast.9), custom_call_target="tpu_custom_call" | custom-call | tf_op jit(solution)/shard_map/finish/pallas_call | solution.py:487
  (2 shorter events, 0.0 us)
Async XLA Ops:
  1.9 7.6 %collective-permute-start = (bf16[112,640]{1,0:T(8,128)(2,1)S(1)}, bf16[112,640]{1,0:T(8,128)(2,1)S(1)}, u32[]{:S(2)}, u32[]{:S(2)}) collective-permute-start(bf16[112,640]{1,0:T(8,128)(2,1)S(1)} %get-tuple-element.14.own_ref), channel_id=1, source_target_pairs={{0,28},{4,0},{8,4},{12,8},{16,12},{20,16},{24,20},{28,24},{1,29},{... | collective-permute-start | bytes 430088 | tf_op jit(solution)/shard_map/ppermute | solution.py:429
  5.3 4.2 %collective-permute-start.1 = (bf16[2,72,128]{2,1,0:T(8,128)(2,1)S(1)}, bf16[2,72,128]{2,1,0:T(8,128)(2,1)S(1)}, u32[]{:S(2)}, u32[]{:S(2)}) collective-permute-start(bf16[2,72,128]{2,1,0:T(8,128)(2,1)S(1)} %get-tuple-element.16.refs_0_.refs_2_), channel_id=1, source_target_pairs={{0,1},{1,0},{2,3},{3,2},{4,5},{5,4},{6,7},{7,6},{8,9},{9,8},{10,11... | collective-permute-start | bytes 110600 | tf_op jit(solution)/shard_map/ppermute | solution.py:431
  6.9 6.2 %collective-permute-start.3 = (bf16[2,72,128]{2,1,0:T(8,128)(2,1)S(1)}, bf16[2,72,128]{2,1,0:T(8,128)(2,1)S(1)}, u32[]{:S(2)}, u32[]{:S(2)}) collective-permute-start(bf16[2,72,128]{2,1,0:T(8,128)(2,1)S(1)} %get-tuple-element.16.refs_0_.refs_2_), channel_id=1, source_target_pairs={{0,3},{1,2},{2,1},{3,0},{4,7},{5,6},{6,5},{7,4},{8,11},{9,10},{10,... | collective-permute-start | bytes 110600 | tf_op jit(solution)/shard_map/ppermute | solution.py:431
  9.4 5.3 %collective-permute-start.2 = (bf16[2,72,128]{2,1,0:T(8,128)(2,1)S(1)}, bf16[2,72,128]{2,1,0:T(8,128)(2,1)S(1)}, u32[]{:S(2)}, u32[]{:S(2)}) collective-permute-start(bf16[2,72,128]{2,1,0:T(8,128)(2,1)S(1)} %get-tuple-element.16.refs_0_.refs_2_), channel_id=1, source_target_pairs={{0,2},{1,3},{2,0},{3,1},{4,6},{5,7},{6,4},{7,5},{8,10},{9,11},{10,... | collective-permute-start | bytes 110600 | tf_op jit(solution)/shard_map/ppermute | solution.py:431
  24.9 11.9 %collective-permute-start.4 = (f32[64,512]{1,0:T(8,128)S(1)}, f32[64,512]{1,0:T(8,128)S(1)}, u32[]{:S(2)}, u32[]{:S(2)}) collective-permute-start(f32[64,512]{1,0:T(8,128)S(1)} %get-tuple-element.20), channel_id=1, source_target_pairs={{0,4},{4,8},{8,12},{12,16},{16,20},{20,24},{24,28},{28,0},{1,5},{5... | collective-permute-start | bytes 393224 | tf_op jit(solution)/shard_map/ppermute | solution.py:485

commit v6 on v5

--- a/solution.py
+++ b/solution.py
@@ -240,10 +240,6 @@
     nt = (((1,), (1,)), ((), ()))
 
     shift_mask(mask_t, shifted)
-    for piece in range(target_t.shape[0] // LANES):
-        lanes = slice(piece * LANES, (piece + 1) * LANES)
-        one = jnp.concatenate([rest_ref[:, lanes], next_ref[rows : rows + half, lanes]], 0)
-        target_t[lanes, :] = jnp.concatenate([one, one], 0).astype(F32).T
     toeplitz = band_maker(ksize, tap_refs, taps32)
     half_fields(ksize, toeplitz, pairs, deep_k, shifted, band, tail_b, fields_b)
 
@@ -267,6 +263,10 @@
         rebuild(0)
         rebuild(1)
 
+        for piece in range(target_t.shape[0] // LANES):
+            lanes = slice(piece * LANES, (piece + 1) * LANES)
+            one = jnp.concatenate([rest_ref[:, lanes], next_ref[rows : rows + half, lanes]], 0)
+            target_t[lanes, :] = jnp.concatenate([one, one], 0).astype(F32).T
         weights = [weight_ref[kernel : kernel + 1, :] for kernel in range(pairs)]
         total_weight = weight_ref[pairs : pairs + 1, :]
         intensity = jnp.zeros((span, window), F32)
@@ -308,11 +308,13 @@
         row = row + jnp.where(lax.broadcasted_iota(jnp.int32, (1, edges), 1) < edges // 2, 0, rows)
         pieces = block // LANES
         spot = piece * window + row
-        spot_hits[...] = (
-            (lax.broadcasted_iota(jnp.int32, (pieces * window, edges), 0) == spot).astype(F32).astype(BF16)
-        )
         slots = slot_hits.shape[0]
-        slot_hits[...] = (lax.broadcasted_iota(jnp.int32, (slots, edges), 0) == slot).astype(F32).astype(BF16)
+
+        def mark(hits, at, of, wanted):
+            count = hits.shape[0] // of
+            place = at * count + lax.broadcasted_iota(jnp.int32, (count, edges), 0)
+            hits[at * count : (at + 1) * count, :] = (place == wanted).astype(F32).astype(BF16)
+
 
         def moved(j):
             return parts[j, GROUP - j : GROUP - j + block, :]
@@ -321,6 +323,8 @@
             products[0:block, deep_k - height : deep_k], tail_a[...], preferred_element_type=F32
         ) + jnp.dot(products[0:block, 2 * deep_k - height :], tail_b[...], preferred_element_type=F32)
         for j in range(0, GROUP, 2):
+            mark(spot_hits, j // 2, GROUP // 2, spot)
+            mark(slot_hits, j // 2, GROUP // 2, slot)
             if j + 2 < GROUP:
                 rebuild(j + 2)
                 rebuild(j + 3)
@@ -337,20 +341,22 @@
             here_ref[:, lanes] = turned[:rows]
             there_ref[:, lanes] = turned[rows:]
 
-        two = jnp.concatenate(split2(jnp.concatenate(tiles_of_total, 1)), 0)
-        picked = jnp.dot(two, spot_hits[...], preferred_element_type=F32)
-        picked = picked[:LANES] + picked[LANES:]
-        col_hit = lax.broadcasted_iota(jnp.int32, (LANES, edges), 0) == col
-        value = jnp.sum(jnp.where(col_hit, picked, 0.0), 0, keepdims=True) * edge_weight
-        tiles = sums_ref.shape[0] // n_sets
-        spread = jnp.where(lax.broadcasted_iota(jnp.int32, (tiles, edges), 0) == owner, value, 0.0)
-        spread = jnp.concatenate([part.astype(F32) for part in split2(spread)], 0).astype(BF16)
-        sums = lax.dot_general(spread, slot_hits[...], nt, preferred_element_type=F32)
-        sums = sums[:tiles] + sums[tiles:]
-        for tile in range(tiles):
-            sums_ref[tile * n_sets : (tile + 1) * n_sets, :] = jnp.broadcast_to(
-                sums[tile : tile + 1], (n_sets, slots)
-            )
+        @pl.when(kern_at >= 0)
+        def _edges():
+            two = jnp.concatenate(split2(jnp.concatenate(tiles_of_total, 1)), 0)
+            picked = jnp.dot(two, spot_hits[...], preferred_element_type=F32)
+            picked = picked[:LANES] + picked[LANES:]
+            col_hit = lax.broadcasted_iota(jnp.int32, (LANES, edges), 0) == col
+            value = jnp.sum(jnp.where(col_hit, picked, 0.0), 0, keepdims=True) * edge_weight
+            tiles = sums_ref.shape[0] // n_sets
+            spread = jnp.where(lax.broadcasted_iota(jnp.int32, (tiles, edges), 0) == owner, value, 0.0)
+            spread = jnp.concatenate([part.astype(F32) for part in split2(spread)], 0).astype(BF16)
+            sums = lax.dot_general(spread, slot_hits[...], nt, preferred_element_type=F32)
+            sums = sums[:tiles] + sums[tiles:]
+            for tile in range(tiles):
+                sums_ref[tile * n_sets : (tile + 1) * n_sets, :] = jnp.broadcast_to(
+                    sums[tile : tile + 1], (n_sets, slots)
+                )
 
 
 def finish_kernel(here_ref, came_ref, got_ref, grad_ref, sums_ref):

time: 37.6 us -> 37.6 us (level)
  no operation moved by 1% of the time
where the time goes in v6:
time: 37.6 us; the launch traced here: 37.4 us
  Pallas kernels  15.7 us (42%)
  blocking collectives  11.8 us (31%)
  starting transfers between devices  7.57 us (20%)
  waiting for transfers between devices  1.55 us (4%)
  between operations  0.68 us (2%)
    all_to_all x1, blocking collectives, on_device(): got = lax.all_to_all(sums, ('tile', 'kern'), 0, 0, tiled=True)  11.8 us
    pallas_call x1, Pallas kernels, on_device(): pl.pallas_call(functools.partial(second_kernel, block, width, ksize, kern...  10.2 us
    ppermute x3, starting transfers between devices, on_device(): lax.ppermute(taps, 'kern', [(i, i ^ step) for i in range(kerns)])  4.17 us
    pallas_call x1, Pallas kernels, on_device(): pl.pallas_call(functools.partial(first_kernel, ksize), out_shape=(jax.Sha...  3.57 us
    ppermute x1, starting transfers between devices, on_device(): lax.ppermute(own, 'tile', [(i, (i - 1) % tiles) for i in range(tiles)])  3.39 us
    ppermute x3, waiting for transfers between devices, on_device(): lax.ppermute(taps, 'kern', [(i, i ^ step) for i in range(kerns)])  1.55 us
    pallas_call x1, Pallas kernels, on_device(): pl.pallas_call(functools.partial(pack_kernel, block), out_shape=(jax.Shap...  1.28 us
  transfers between devices with their start and end apart: 5, of which 1 were waited for; matrix products, arithmetic and copies ran while one was open for 0% of the time, Pallas kernels for 10%

profile of v6, /device:TPU:0, one launch (start us, length us, event | category | flops | bytes accessed | tf_op | source)
XLA Modules:
  0.0 37.4 jit_solution(3610722781417403059)
XLA Ops:
  0.6 1.3 %pack.1 = (bf16[112,640]{1,0:T(8,128)(2,1)S(1)}, bf16[32,640]{1,0:T(8,128)(2,1)S(1)}, bf16[2,72,128]{2,1,0:T(8,128)(2,1)S(1)}, f32[8,128]{1,0:T(8,128)S(1)}) custom-call(bf16[64,2048]{1,0:T(8,128)(2,1)} %mask_hbm.1, s32[64,2048]{1,0:T(8,128)} %target_hbm.1, bf16[1,65,65]{2,1,0:T(8,128)(2,1)} %real_hbm.1, bf16[1,65,65]{2,1,0:T(8,128)(2,1)} %imag_hbm.1, ...), custom_call_target="tpu_custom_call" | custom-call | tf_op jit(solution)/shard_map/pack/pallas_call | solution.py:393
  1.9 3.4 %collective-permute-start = (bf16[112,640]{1,0:T(8,128)(2,1)S(1)}, bf16[112,640]{1,0:T(8,128)(2,1)S(1)}, u32[]{:S(2)}, u32[]{:S(2)}) collective-permute-start(bf16[112,640]{1,0:T(8,128)(2,1)S(1)} %get-tuple-element.14.own_ref), channel_id=1, source_target_pairs={{0,28},{4,0},{8,4},{12,8},{16,12},{20,16},{24,20},{28,24},{1,29},{... | collective-permute-start | bytes 430088 | tf_op jit(solution)/shard_map/ppermute | solution.py:435
  5.3 1.6 %collective-permute-start.1 = (bf16[2,72,128]{2,1,0:T(8,128)(2,1)S(1)}, bf16[2,72,128]{2,1,0:T(8,128)(2,1)S(1)}, u32[]{:S(2)}, u32[]{:S(2)}) collective-permute-start(bf16[2,72,128]{2,1,0:T(8,128)(2,1)S(1)} %get-tuple-element.16.refs_0_.refs_2_), channel_id=1, source_target_pairs={{0,1},{1,0},{2,3},{3,2},{4,5},{5,4},{6,7},{7,6},{8,9},{9,8},{10,11... | collective-permute-start | bytes 110600 | tf_op jit(solution)/shard_map/ppermute | solution.py:437
  6.9 2.5 %collective-permute-start.3 = (bf16[2,72,128]{2,1,0:T(8,128)(2,1)S(1)}, bf16[2,72,128]{2,1,0:T(8,128)(2,1)S(1)}, u32[]{:S(2)}, u32[]{:S(2)}) collective-permute-start(bf16[2,72,128]{2,1,0:T(8,128)(2,1)S(1)} %get-tuple-element.16.refs_0_.refs_2_), channel_id=1, source_target_pairs={{0,3},{1,2},{2,1},{3,0},{4,7},{5,6},{6,5},{7,4},{8,11},{9,10},{10,... | collective-permute-start | bytes 110600 | tf_op jit(solution)/shard_map/ppermute | solution.py:437
  9.4 0.1 collective-permute-start.2
  9.5 0.0 collective-permute-done.1.refs_1_.refs_3_
  9.5 0.0 collective-permute-done.next_ref
  9.5 3.6 %first.1 = (f32[640,128]{1,0:T(8,128)S(1)}, f32[576,256]{1,0:T(8,128)S(1)}) custom-call(bf16[112,640]{1,0:T(8,128)(2,1)S(1)} %get-tuple-element.14.own_ref, bf16[112,640]{1,0:T(8,128)(2,1)S(1)} %collective-permute-done.next_ref, bf16[2,72,128]{2,1,0:T(8,128)(2,1)S(1)} %get-tuple-element.16.refs_0_.refs_2_, ...), custom_call_target="tpu_custom_call" | custom-call | flops 2453667840 | bytes 589824 | tf_op jit(solution)/shard_map/first/pallas_call | solution.py:446
  13.1 0.0 collective-permute-done.3.refs_5_
  13.1 1.5 %collective-permute-done.2.refs_4_ = bf16[2,72,128]{2,1,0:T(8,128)(2,1)S(1)} collective-permute-done((bf16[2,72,128]{2,1,0:T(8,128)(2,1)S(1)}, bf16[2,72,128]{2,1,0:T(8,128)(2,1)S(1)}, u32[]{:S(2)}, u32[]{:S(2)}) %collective-permute-start.2) | collective-permute-done | bytes 36896 | tf_op jit(solution)/shard_map/ppermute | solution.py:437
  14.6 10.2 %fields.1 = (f32[64,512]{1,0:T(8,128)S(1)}, f32[64,512]{1,0:T(8,128)S(1)}, f32[32,256]{1,0:T(8,128)S(1)}) custom-call(f32[8,128]{1,0:T(8,128)S(1)} %get-tuple-element.13.weight_ref, bf16[112,640]{1,0:T(8,128)(2,1)S(1)} %get-tuple-element.14.own_ref, bf16[112,640]{1,0:T(8,128)(2,1)S(1)} %collective-permute-done.next_ref, ...), custom_call_target="tpu_custom_call" | custom-call | flops 7361003520 | bytes 589824 | tf_op jit(solution)/shard_map/fields/pallas_call | solution.py:464
  24.8 0.0 collective-permute-start.4
  24.9 11.8 %all_to_all.11 = f32[32,1,256]{2,1,0:T(1,128)S(1)} all-to-all(f32[32,1,256]{2,1,0:T(1,128)S(1)} %copy.11), channel_id=1, replica_groups=mesh['tile'=8,'kern'=4] {'tile','kern'}, dimensions={0} | all-to-all | bytes 65536 | tf_op jit(solution)/shard_map/all_to_all | solution.py:492
  36.7 0.0 collective-permute-done.4.came_ref
  36.7 0.7 %finish.1 = (f32[64,512]{1,0:T(8,128)}, f32[1,256]{1,0:T(1,128)}) custom-call(f32[64,512]{1,0:T(8,128)S(1)} %get-tuple-element.19.here_ref, f32[64,512]{1,0:T(8,128)S(1)} %collective-permute-done.4.came_ref, f32[32,256]{1,0:T(8,128)S(1)} %bitcast.9), custom_call_target="tpu_custom_call" | custom-call | tf_op jit(solution)/shard_map/finish/pallas_call | solution.py:493
  (2 shorter events, 0.0 us)
Async XLA Ops:
  1.9 7.6 %collective-permute-start = (bf16[112,640]{1,0:T(8,128)(2,1)S(1)}, bf16[112,640]{1,0:T(8,128)(2,1)S(1)}, u32[]{:S(2)}, u32[]{:S(2)}) collective-permute-start(bf16[112,640]{1,0:T(8,128)(2,1)S(1)} %get-tuple-element.14.own_ref), channel_id=1, source_target_pairs={{0,28},{4,0},{8,4},{12,8},{16,12},{20,16},{24,20},{28,24},{1,29},{... | collective-permute-start | bytes 430088 | tf_op jit(solution)/shard_map/ppermute | solution.py:435
  5.3 4.2 %collective-permute-start.1 = (bf16[2,72,128]{2,1,0:T(8,128)(2,1)S(1)}, bf16[2,72,128]{2,1,0:T(8,128)(2,1)S(1)}, u32[]{:S(2)}, u32[]{:S(2)}) collective-permute-start(bf16[2,72,128]{2,1,0:T(8,128)(2,1)S(1)} %get-tuple-element.16.refs_0_.refs_2_), channel_id=1, source_target_pairs={{0,1},{1,0},{2,3},{3,2},{4,5},{5,4},{6,7},{7,6},{8,9},{9,8},{10,11... | collective-permute-start | bytes 110600 | tf_op jit(solution)/shard_map/ppermute | solution.py:437
  6.9 6.2 %collective-permute-start.3 = (bf16[2,72,128]{2,1,0:T(8,128)(2,1)S(1)}, bf16[2,72,128]{2,1,0:T(8,128)(2,1)S(1)}, u32[]{:S(2)}, u32[]{:S(2)}) collective-permute-start(bf16[2,72,128]{2,1,0:T(8,128)(2,1)S(1)} %get-tuple-element.16.refs_0_.refs_2_), channel_id=1, source_target_pairs={{0,3},{1,2},{2,1},{3,0},{4,7},{5,6},{6,5},{7,4},{8,11},{9,10},{10,... | collective-permute-start | bytes 110600 | tf_op jit(solution)/shard_map/ppermute | solution.py:437
  9.4 5.3 %collective-permute-start.2 = (bf16[2,72,128]{2,1,0:T(8,128)(2,1)S(1)}, bf16[2,72,128]{2,1,0:T(8,128)(2,1)S(1)}, u32[]{:S(2)}, u32[]{:S(2)}) collective-permute-start(bf16[2,72,128]{2,1,0:T(8,128)(2,1)S(1)} %get-tuple-element.16.refs_0_.refs_2_), channel_id=1, source_target_pairs={{0,2},{1,3},{2,0},{3,1},{4,6},{5,7},{6,4},{7,5},{8,10},{9,11},{10,... | collective-permute-start | bytes 110600 | tf_op jit(solution)/shard_map/ppermute | solution.py:437
  24.8 11.9 %collective-permute-start.4 = (f32[64,512]{1,0:T(8,128)S(1)}, f32[64,512]{1,0:T(8,128)S(1)}, u32[]{:S(2)}, u32[]{:S(2)}) collective-permute-start(f32[64,512]{1,0:T(8,128)S(1)} %get-tuple-element.20), channel_id=1, source_target_pairs={{0,4},{4,8},{8,12},{12,16},{16,20},{20,24},{24,28},{28,0},{1,5},{5... | collective-permute-start | bytes 393224 | tf_op jit(solution)/shard_map/ppermute | solution.py:491
